TPU v7x, 256 devices: a whole 4x4x8 slice. The times are simulated.
256 devices in a mesh: ctx: 64 (over z, y_lo, x), tp: 4 (over y_hi, core).
Axes of the slice: x: 4, y: 4 (y_hi: 2, y_lo: 2; y = y_hi * 2 + y_lo), z: 8, core: 2. Of those that a mesh axis runs over, the one named last changes fastest.
Arguments:
- queries: bfloat16 [16384, 8192], P('ctx', 'tp'), may hold values from -6 to 6
- key_proj: bfloat16 [16384, 8192], P('ctx', 'tp'), may hold values from -6 to 6
- values: bfloat16 [16384, 8192], P('ctx', 'tp'), may hold values from -6 to 6
- residues: float32 [16, 8192], P(None, 'tp'), may hold values from -0.4 to 0.4
- decay_rates: float32 [16, 8192], P(None, 'tp'), may hold values from 0 to 0.034, as said below
- skip_weight: float32 [8192], P('tp'), may hold values from 0.5 to 1.5
- stream: bfloat16 [16384, 8192], P('ctx', 'tp'), may hold values from -110 to 110
- norm_gain: float32 [8192], P('tp'), may hold values from 0.1 to 1.9
Outputs:
- new_stream: bfloat16 [16384, 8192], P('ctx', 'tp')
- normed: bfloat16 [16384, 8192], P('ctx', 'tp')
Inputs may be any that keep to these rules, and one draw needn't show every extreme that they name: `decay_rates`: each mode's decay per position; all positive.
All inputs are finite; a program needn't handle non-finite values.
Results may differ from a plain program's by a relative error of at most 0.007.
Values may be sent and summed in bfloat16 or wider, within the bound.
No kernel may reach another device: no remote copies, remote signals or barrier semaphores. Data moves between devices by JAX's collectives and lax.ppermute only.
A program may use at most 128 MiB of HBM per device.

v0:
```python
import functools

import jax
import jax.numpy as jnp
from jax import lax
from jax.experimental import pallas as pl
from jax.experimental.pallas import tpu as pltpu
from jax.sharding import PartitionSpec as P

epsilon = 1e-06
lanes = 128
sublanes = 8
piece_width = 512
vmem_bytes = 24 * 1024 * 1024


def at_group(group):
    return pl.ds(pl.multiple_of(group * lanes, lanes), lanes)


def spread(ref, mode, cols):
    return jnp.broadcast_to(ref[pl.ds(mode, 1), cols], (sublanes, lanes))


def tree_sum(parts):
    parts = list(parts)
    while len(parts) > 1:
        parts = [l + r for l, r in zip(parts[::2], parts[1::2])]
    return parts[0]


def state_kernel(
    span, q_hbm, k_hbm, v_hbm, x_hbm, decay_hbm, res_hbm, skip_hbm,
    total_ref, sent_ref, chunk_ref, sig_ref, v_ref, x_ref, decay_ref, res_ref, skip_ref,
    q_ref, k_ref, rows_ref, pair_sem, side_sem,
):
    modes = decay_ref.shape[0]
    rows, width = q_ref.shape
    pieces = width // piece_width
    pair = []
    first = pltpu.make_async_copy(decay_hbm, decay_ref, side_sem.at[0])
    first.start()
    for p in range(pieces):
        cols = pl.ds(p * piece_width, piece_width)
        for at, (src, dst) in enumerate(((q_hbm, q_ref), (k_hbm, k_ref))):
            pair.append(pltpu.make_async_copy(src.at[:, cols], dst.at[:, cols], pair_sem.at[at, p]))
            pair[-1].start()
    side = []
    for at, (src, dst) in enumerate(((v_hbm, v_ref), (x_hbm, x_ref), (res_hbm, res_ref), (skip_hbm, skip_ref))):
        side.append(pltpu.make_async_copy(src, dst, side_sem.at[at + 1]))
        side[-1].start()
    run = lax.broadcasted_iota(jnp.int32, (sublanes, lanes), 0)
    left = ((sublanes - 1 - run) * span).astype(jnp.float32)
    first.wait()
    for p in range(pieces):
        pair[2 * p].wait()
        pair[2 * p + 1].wait()

        @pl.loop(p * piece_width // lanes, (p + 1) * piece_width // lanes)
        def _(group):
            cols = at_group(group)
            product = q_ref[:, cols].astype(jnp.float32) * k_ref[:, cols].astype(jnp.float32)
            rows_ref[...] = product.astype(jnp.bfloat16).astype(jnp.float32)
            decays = [spread(decay_ref, n, cols) for n in range(modes)]
            steps = [jnp.exp(-d) for d in decays]
            states = None
            for j in range(span):
                sig = rows_ref[pl.ds(j, sublanes, stride=span), :]
                sig_ref[pl.ds(j * sublanes, sublanes), cols] = sig
                states = [s * a + sig for s, a in zip(states, steps)] if j else [sig] * modes
            for n in range(modes):
                chunk_ref[n, :, cols] = states[n]
                weighted = states[n] * jnp.exp(-decays[n] * left)
                total_ref[pl.ds(n, 1), cols] = jnp.sum(weighted, axis=0, keepdims=True)
            sent_ref[:, cols] = total_ref[:, cols].astype(jnp.bfloat16)

    for copy in side:
        copy.wait()


def local_kernel(span, piece, decay_ref, res_ref, skip_ref, sig_ref, chunk_ref, v_ref, x_ref, base_ref, conv_ref):
    modes = decay_ref.shape[0]
    run = lax.broadcasted_iota(jnp.int32, (sublanes, lanes), 0)

    def shifted(state, by):
        return jnp.where(run >= by, pltpu.roll(state, by, 0), 0.0)

    @pl.loop(0, piece_width // lanes)
    def _(group):
        cols = at_group(group + piece * (piece_width // lanes))
        skip = jnp.broadcast_to(skip_ref[:, cols], (sublanes, lanes))
        half = modes // 2
        for low in range(0, modes, half):
            steps, gains, states = [], [], []
            for n in range(low, low + half):
                decay = spread(decay_ref, n, cols)
                gain = spread(res_ref, n, cols)
                state = chunk_ref[n, :, cols]
                over = jnp.exp(decay * float(-span))
                for by in (1, 2, 4):
                    state = state + over * shifted(state, by)
                    over = over * over
                states.append(gain * shifted(state, 1))
                steps.append(jnp.exp(-decay))
                gains.append(gain)
            for j in range(span):
                sig = sig_ref[pl.ds(j * sublanes, sublanes), cols]
                states = [s * a + sig * g for s, a, g in zip(states, steps, gains)]
                out = conv_ref.at[pl.ds(j, sublanes, stride=span), :]
                if low == 0:
                    out[...] = tree_sum(states) + skip * sig
                else:
                    out[...] = out[...] + tree_sum(states)
        mixed = v_ref[:, cols].astype(jnp.float32) * conv_ref[...]
        base_ref[:, at_group(group)] = x_ref[:, cols].astype(jnp.float32) + mixed


def merge_kernel(size, rows, last, arrived_ref, decay_ref, *rest):
    if size == 1:
        total_ref, rest = rest[0], rest[1:]
    elif last:
        enter_ref, rest = rest[0], rest[1:]
    else:
        total_ref, enter_ref, rest = rest[0], rest[1], rest[2:]
    position = lax.axis_index("ctx")
    arrived = arrived_ref[...].astype(jnp.float32)
    decay = decay_ref[...]
    upper = (position & size) != 0
    within = (position & (size - 1)).astype(jnp.float32) * float(rows)
    share = jnp.where(upper, arrived, 0.0) * jnp.exp(decay * -within)
    rest[0][...] = share if size == 1 else enter_ref[...] + share
    if not last:
        over = jnp.exp(decay * float(-rows * size))
        total = total_ref[...]
        total = jnp.where(upper, total + over * arrived, over * total + arrived)
        rest[1][...] = total
        rest[2][...] = total.astype(jnp.bfloat16)


def finish_kernel(enter_ref, decay_ref, res_ref, v_ref, *rest):
    base_refs = rest[:-3]
    new_ref, power_ref, acc_ref = rest[-3:]
    modes = decay_ref.shape[0]
    rows = v_ref.shape[0]
    run = lax.broadcasted_iota(jnp.int32, (sublanes, lanes), 0)
    ahead = (run + 1).astype(jnp.float32)
    acc_ref[...] = jnp.zeros_like(acc_ref)
    for piece, base_ref in enumerate(base_refs):

        @pl.loop(0, piece_width // lanes)
        def _(group):
            here = at_group(group)
            cols = at_group(group + piece * (piece_width // lanes))
            steps, states = [], []
            for n in range(modes):
                decay = spread(decay_ref, n, cols)
                start = spread(res_ref, n, cols) * spread(enter_ref, n, cols)
                states.append(start * jnp.exp(-decay * ahead))
                steps.append(jnp.exp(decay * float(-sublanes)))
            for pair in range(rows // (2 * sublanes)):
                halves = []
                for half in range(2):
                    halves.append(tree_sum(states))
                    states = [s * a for s, a in zip(states, steps)]
                at = pl.ds(pair * 2 * sublanes, 2 * sublanes)
                carried = jnp.concatenate(halves, axis=0)
                fresh = base_ref[at, here] + v_ref[at, cols].astype(jnp.float32) * carried
                fresh = fresh.astype(jnp.bfloat16)
                new_ref[at, cols] = fresh
                fresh = fresh.astype(jnp.float32)
                acc_ref[at, :] += fresh * fresh

    ones = jnp.ones((sublanes, lanes), jnp.float32)
    sums = lax.dot_general(
        ones,
        acc_ref[...],
        (((1,), (1,)), ((), ())),
        precision=lax.Precision.HIGHEST,
        preferred_element_type=jnp.float32,
    )
    power_ref[...] = sums[0:1]


def norm_kernel(channels, mine_ref, other_ref, gain_ref, new_ref, out_hbm, inv_ref, out_ref, sem):
    rows, width = new_ref.shape
    power = (mine_ref[...] + other_ref[...]) * (1.0 / channels)
    inverse = lax.rsqrt(power + epsilon)
    inv_ref[...] = jnp.transpose(jnp.broadcast_to(inverse, (lanes, rows)))
    copies = []
    for p in range(width // piece_width):

        @pl.loop(p * piece_width // lanes, (p + 1) * piece_width // lanes)
        def _(group):
            cols = at_group(group)
            scaled = new_ref[:, cols].astype(jnp.float32) * inv_ref[...] * gain_ref[:, cols]
            out_ref[:, cols] = scaled.astype(jnp.bfloat16)

        cols = pl.ds(p * piece_width, piece_width)
        copies.append(pltpu.make_async_copy(out_ref.at[:, cols], out_hbm.at[:, cols], sem.at[p]))
        copies[-1].start()
    for copy in copies:
        copy.wait()


def shards(queries, key_proj, values, residues, decay_rates, skip_weight, stream, norm_gain):
    rows, width = queries.shape
    modes = decay_rates.shape[0]
    span = rows // sublanes
    params = pltpu.CompilerParams(vmem_limit_bytes=vmem_bytes)
    f32, bf16 = jnp.float32, jnp.bfloat16
    in_vmem = pl.BlockSpec(memory_space=pltpu.VMEM)
    anywhere = pl.BlockSpec(memory_space=pl.ANY)
    pieces = width // piece_width

    far = [queries, key_proj, values, stream, decay_rates, residues, skip_weight[None, :]]
    far = [pltpu.with_memory_space_constraint(a, pltpu.HBM) for a in far]
    outs = [
        ((modes, width), f32),
        ((modes, width), bf16),
        ((modes, sublanes, width), f32),
        ((rows, width), f32),
        ((rows, width), bf16),
        ((rows, width), bf16),
        ((modes, width), f32),
        ((modes, width), f32),
        ((1, width), f32),
    ]
    total, sent, chunks, signal, near_values, near_stream, decay, gains, skip = pl.pallas_call(
        functools.partial(state_kernel, span),
        in_specs=[anywhere] * len(far),
        out_specs=[in_vmem] * len(outs),
        out_shape=[pltpu.VMEM(shape, dtype) for shape, dtype in outs],
        scratch_shapes=[
            pltpu.VMEM((rows, width), bf16),
            pltpu.VMEM((rows, width), bf16),
            pltpu.VMEM((rows, lanes), f32),
            pltpu.SemaphoreType.DMA((2, pieces)),
            pltpu.SemaphoreType.DMA((5,)),
        ],
        compiler_params=params,
        cost_estimate=pl.CostEstimate(flops=2 * modes * rows * width, bytes_accessed=4 * rows * width, transcendentals=0),
        name="states",
    )(*far)

    def local_piece(piece, decay):
        return pl.pallas_call(
            functools.partial(local_kernel, span, piece),
            in_specs=[in_vmem] * 7,
            out_specs=in_vmem,
            out_shape=pltpu.VMEM((rows, piece_width), f32),
            scratch_shapes=[pltpu.VMEM((rows, lanes), f32)],
            compiler_params=params,
            cost_estimate=pl.CostEstimate(
                flops=4 * modes * rows * piece_width, bytes_accessed=12 * rows * piece_width, transcendentals=0
            ),
            name="local",
        )(decay, gains, skip, signal, chunks, near_values, near_stream)

    def link(partner_of):
        places = [(z, y, x) for z in range(8) for y in range(2) for x in range(4)]
        index = lambda z, y, x: (z * 2 + y) * 4 + x
        return [(index(*at), index(*partner_of(*at))) for at in places]

    rounds = [
        link(lambda z, y, x: (z, y, x ^ 1)),
        link(lambda z, y, x: (z, y, x ^ 3)),
        link(lambda z, y, x: (z, y ^ 1, x)),
        link(lambda z, y, x: (z ^ 1, y, x)),
        link(lambda z, y, x: (z ^ 2, y, x)),
        link(lambda z, y, x: (7 - z, y, x)),
    ]
    def merge(size, last, arrived, total, enter):
        operands = [arrived, decay] + ([] if last else [total]) + ([] if size == 1 else [enter])
        outs = [f32] if last else [f32, f32, bf16]
        return pl.pallas_call(
            functools.partial(merge_kernel, size, rows, last),
            in_specs=[in_vmem] * len(operands),
            out_specs=[in_vmem] * len(outs),
            out_shape=[pltpu.VMEM((modes, width), dtype) for dtype in outs],
            compiler_params=params,
            name="merge",
        )(*operands)

    enter = None
    bases = []
    for level, pairs in enumerate(rounds):
        arrived = lax.ppermute(sent, "ctx", pairs)
        if level < pieces:
            tied, sent = lax.optimization_barrier((decay, sent))
            base = local_piece(level, tied)
            arrived, base = lax.optimization_barrier((arrived, base))
            bases.append(base)
        if level + 1 < len(rounds):
            enter, total, sent = merge(1 << level, False, arrived, total, enter)
        else:
            (enter,) = merge(1 << level, True, arrived, None, enter)

    fresh, power = pl.pallas_call(
        finish_kernel,
        in_specs=[in_vmem] * (4 + pieces),
        out_specs=[in_vmem] * 2,
        out_shape=[pltpu.VMEM((rows, width), bf16), pltpu.VMEM((1, rows), f32)],
        scratch_shapes=[pltpu.VMEM((rows, lanes), f32)],
        compiler_params=params,
        cost_estimate=pl.CostEstimate(flops=2 * modes * rows * width, bytes_accessed=8 * rows * width, transcendentals=0),
        name="finish",
    )(enter, decay, gains, near_values, *bases)

    power = power + lax.ppermute(power, "tp", [(i, i ^ 1) for i in range(4)])
    other = lax.ppermute(power, "tp", [(i, i ^ 3) for i in range(4)])

    channels = width * lax.axis_size("tp")
    normed = pl.pallas_call(
        functools.partial(norm_kernel, channels),
        in_specs=[in_vmem] * 4,
        out_specs=anywhere,
        out_shape=pltpu.HBM((rows, width), bf16),
        scratch_shapes=[
            pltpu.VMEM((rows, lanes), f32),
            pltpu.VMEM((rows, width), bf16),
            pltpu.SemaphoreType.DMA((pieces,)),
        ],
        compiler_params=params,
        name="normalise",
    )(power, other, norm_gain[None, :], fresh)
    return (fresh, normed)


def solution(mesh):
    in_specs = (
        P("ctx", "tp"),
        P("ctx", "tp"),
        P("ctx", "tp"),
        P(None, "tp"),
        P(None, "tp"),
        P("tp"),
        P("ctx", "tp"),
        P("tp"),
    )
    out_specs = (P("ctx", "tp"), P("ctx", "tp"))
    return jax.shard_map(shards, mesh=mesh, in_specs=in_specs, out_specs=out_specs, check_vma=False)
```

profile of v0, /device:TPU:1, one launch (start us, length us, event | category | flops | bytes accessed | tf_op | source)
XLA Modules:
  0.0 52.0 jit_solution(2532815168335557890)
XLA Ops:
  0.6 5.3 %states.1 = (f32[16,2048]{1,0:T(8,128)S(1)}, bf16[16,2048]{1,0:T(8,128)(2,1)S(1)}, f32[16,8,2048]{2,1,0:T(8,128)S(1)}, f32[256,2048]{1,0:T(8,128)S(1)}, bf16[256...) custom-call(bf16[256,2048]{1,0:T(8,128)(2,1)} %q_hbm.1, ...), custom_call_target="tpu_custom_call" | custom-call | flops 16777216 | bytes 2097152 | tf_op jit(solution)/shard_map/states/pallas_call | solution.py:228
  6.0 2.1 %collective-permute-start = (bf16[16,2048]{1,0:T(8,128)(2,1)S(1)}, bf16[16,2048]{1,0:T(8,128)(2,1)S(1)}, u32[]{:S(2)}, u32[]{:S(2)}) collective-permute-start(bf16[16,2048]{1,0:T(8,128)(2,1)S(1)} %get-tuple-element.39), channel_id=1, source_target_pairs={{0,4},{4,0},{8,12},{12,8},{16,20},{20,16},{24,28},{28,24},{32,36},... | collective-permute-start | bytes 196616 | tf_op jit(solution)/shard_map/ppermute | solution.py:287
  8.1 1.8 %local.4.rest_0_ = f32[256,512]{1,0:T(8,128)S(1)} custom-call(f32[16,2048]{1,0:T(8,128)S(1)} %get-tuple-element.61.decay_ref, f32[16,2048]{1,0:T(8,128)S(1)} %get-tuple-element.42.res_ref, f32[1,2048]{1,0:T(1,128)S(1)} %get-tuple-element.43.skip_ref, f32[256,2048]{1,0:T(8,128)S(1)} %get-tuple-element.44.sig_ref, ...), custom_call_target="tpu_custom_call" | custom-call | flops 8388608 | bytes 1572864 | tf_op jit(solution)/shard_map/local/pallas_call | solution.py:246
  9.9 0.0 collective-permute-done.arrived_ref
  9.9 0.1 merge.6
  10.0 2.7 %collective-permute-start.1 = (bf16[16,2048]{1,0:T(8,128)(2,1)S(1)}, bf16[16,2048]{1,0:T(8,128)(2,1)S(1)}, u32[]{:S(2)}, u32[]{:S(2)}) collective-permute-start(bf16[16,2048]{1,0:T(8,128)(2,1)S(1)} %get-tuple-element.50), channel_id=1, source_target_pairs={{0,12},{4,8},{8,4},{12,0},{16,28},{20,24},{24,20},{28,16},{32,44},... | collective-permute-start | bytes 196616 | tf_op jit(solution)/shard_map/ppermute | solution.py:287
  12.6 1.8 %local.5.rest_1_ = f32[256,512]{1,0:T(8,128)S(1)} custom-call(f32[16,2048]{1,0:T(8,128)S(1)} %get-tuple-element.61.decay_ref, f32[16,2048]{1,0:T(8,128)S(1)} %get-tuple-element.42.res_ref, f32[1,2048]{1,0:T(1,128)S(1)} %get-tuple-element.43.skip_ref, f32[256,2048]{1,0:T(8,128)S(1)} %get-tuple-element.44.sig_ref, ...), custom_call_target="tpu_custom_call" | custom-call | flops 8388608 | bytes 1572864 | tf_op jit(solution)/shard_map/local/pallas_call | solution.py:246
  14.4 0.0 collective-permute-done.1.arrived_ref
  14.4 0.1 merge.7
  14.5 1.4 %collective-permute-start.2 = (bf16[16,2048]{1,0:T(8,128)(2,1)S(1)}, bf16[16,2048]{1,0:T(8,128)(2,1)S(1)}, u32[]{:S(2)}, u32[]{:S(2)}) collective-permute-start(bf16[16,2048]{1,0:T(8,128)(2,1)S(1)} %get-tuple-element.55), channel_id=1, source_target_pairs={{0,16},{4,20},{8,24},{12,28},{16,0},{20,4},{24,8},{28,12},{32,48},... | collective-permute-start | bytes 196616 | tf_op jit(solution)/shard_map/ppermute | solution.py:287
  16.0 1.8 %local.6.rest_2_ = f32[256,512]{1,0:T(8,128)S(1)} custom-call(f32[16,2048]{1,0:T(8,128)S(1)} %get-tuple-element.61.decay_ref, f32[16,2048]{1,0:T(8,128)S(1)} %get-tuple-element.42.res_ref, f32[1,2048]{1,0:T(1,128)S(1)} %get-tuple-element.43.skip_ref, f32[256,2048]{1,0:T(8,128)S(1)} %get-tuple-element.44.sig_ref, ...), custom_call_target="tpu_custom_call" | custom-call | flops 8388608 | bytes 1572864 | tf_op jit(solution)/shard_map/local/pallas_call | solution.py:246
  17.7 0.0 collective-permute-done.2.arrived_ref
  17.7 0.1 merge.8
  17.8 1.8 %collective-permute-start.3 = (bf16[16,2048]{1,0:T(8,128)(2,1)S(1)}, bf16[16,2048]{1,0:T(8,128)(2,1)S(1)}, u32[]{:S(2)}, u32[]{:S(2)}) collective-permute-start(bf16[16,2048]{1,0:T(8,128)(2,1)S(1)} %get-tuple-element.60), channel_id=1, source_target_pairs={{0,32},{4,36},{8,40},{12,44},{16,48},{20,52},{24,56},{28,60},{32,0... | collective-permute-start | bytes 196616 | tf_op jit(solution)/shard_map/ppermute | solution.py:287
  19.6 1.8 %local.7.rest_3_ = f32[256,512]{1,0:T(8,128)S(1)} custom-call(f32[16,2048]{1,0:T(8,128)S(1)} %get-tuple-element.61.decay_ref, f32[16,2048]{1,0:T(8,128)S(1)} %get-tuple-element.42.res_ref, f32[1,2048]{1,0:T(1,128)S(1)} %get-tuple-element.43.skip_ref, f32[256,2048]{1,0:T(8,128)S(1)} %get-tuple-element.44.sig_ref, ...), custom_call_target="tpu_custom_call" | custom-call | flops 8388608 | bytes 1572864 | tf_op jit(solution)/shard_map/local/pallas_call | solution.py:246
  21.3 0.0 collective-permute-done.3.arrived_ref
  21.4 0.1 merge.9
  21.4 3.2 %collective-permute-start.4 = (bf16[16,2048]{1,0:T(8,128)(2,1)S(1)}, bf16[16,2048]{1,0:T(8,128)(2,1)S(1)}, u32[]{:S(2)}, u32[]{:S(2)}) collective-permute-start(bf16[16,2048]{1,0:T(8,128)(2,1)S(1)} %get-tuple-element.65), channel_id=1, source_target_pairs={{0,64},{4,68},{8,72},{12,76},{16,80},{20,84},{24,88},{28,92},{32,9... | collective-permute-start | bytes 196616 | tf_op jit(solution)/shard_map/ppermute | solution.py:287
  24.7 1.7 %collective-permute-done.4.arrived_ref = bf16[16,2048]{1,0:T(8,128)(2,1)S(1)} collective-permute-done((bf16[16,2048]{1,0:T(8,128)(2,1)S(1)}, bf16[16,2048]{1,0:T(8,128)(2,1)S(1)}, u32[]{:S(2)}, u32[]{:S(2)}) %collective-permute-start.4) | collective-permute-done | bytes 65568 | tf_op jit(solution)/shard_map/ppermute | solution.py:287
  26.3 0.7 %merge.10 = (f32[16,2048]{1,0:T(8,128)S(1)}, f32[16,2048]{1,0:T(8,128)}, bf16[16,2048]{1,0:T(8,128)(2,1)S(1)}) custom-call(bf16[16,2048]{1,0:T(8,128)(2,1)S(1)} %collective-permute-done.4.arrived_ref, f32[16,2048]{1,0:T(8,128)S(1)} %get-tuple-element.61.decay_ref, f32[16,2048]{1,0:T(8,128)S(1)} %get-tuple-element.66.rest_0_, ...), custom_call_target="tpu_custom_call" | custom-call | tf_op jit(solution)/shard_map/merge/pallas_call | solution.py:275
  27.0 5.5 %collective-permute-start.5 = (bf16[16,2048]{1,0:T(8,128)(2,1)S(1)}, bf16[16,2048]{1,0:T(8,128)(2,1)S(1)}, u32[]{:S(2)}, u32[]{:S(2)}) collective-permute-start(bf16[16,2048]{1,0:T(8,128)(2,1)S(1)} %get-tuple-element.68), channel_id=1, source_target_pairs={{0,224},{4,228},{8,232},{12,236},{16,240},{20,244},{24,248},{28,25... | collective-permute-start | bytes 196616 | tf_op jit(solution)/shard_map/ppermute | solution.py:287
  32.5 2.3 %collective-permute-done.5.arrived_ref = bf16[16,2048]{1,0:T(8,128)(2,1)S(1)} collective-permute-done((bf16[16,2048]{1,0:T(8,128)(2,1)S(1)}, bf16[16,2048]{1,0:T(8,128)(2,1)S(1)}, u32[]{:S(2)}, u32[]{:S(2)}) %collective-permute-start.5) | collective-permute-done | bytes 65568 | tf_op jit(solution)/shard_map/ppermute | solution.py:287
  34.9 0.0 copy-start
  34.9 3.2 %finish.1 = (bf16[256,2048]{1,0:T(8,128)(2,1)S(1)}, f32[1,256]{1,0:T(1,128)S(1)}) custom-call(f32[16,2048]{1,0:T(8,128)S(1)} %merge.11.enter_ref, f32[16,2048]{1,0:T(8,128)S(1)} %get-tuple-element.61.decay_ref, f32[16,2048]{1,0:T(8,128)S(1)} %get-tuple-element.42.res_ref, bf16[256,2048]{1,0:T(8,128)(2,1)S(1)} %get-tuple-element.46.v_ref, ...), custom_call_target="tpu_custom_call" | custom-call | flops 16777216 | bytes 4194304 | tf_op jit(solution)/shard_map/finish/pallas_call | solution.py:298
  38.1 7.2 %collective-permute-start.6 = (f32[1,256]{1,0:T(1,128)S(1)}, f32[1,256]{1,0:T(1,128)S(1)}, u32[]{:S(2)}, u32[]{:S(2)}) collective-permute-start(f32[1,256]{1,0:T(1,128)S(1)} %get-tuple-element.75), channel_id=1, source_target_pairs={{0,1},{1,0},{2,3},{3,2},{4,5},{5,4},{6,7},{7,6},{8,9},{9,8},{10,11... | collective-permute-start | bytes 3080 | tf_op jit(solution)/shard_map/ppermute | solution.py:309
  45.3 0.8 %collective-permute-done.6 = f32[1,256]{1,0:T(1,128)S(1)} collective-permute-done((f32[1,256]{1,0:T(1,128)S(1)}, f32[1,256]{1,0:T(1,128)S(1)}, u32[]{:S(2)}, u32[]{:S(2)}) %collective-permute-start.6) | collective-permute-done | bytes 1056 | tf_op jit(solution)/shard_map/ppermute | solution.py:309
  46.2 3.1 %collective-permute-start.7 = (f32[1,256]{1,0:T(1,128)S(1)}, f32[1,256]{1,0:T(1,128)S(1)}, u32[]{:S(2)}, u32[]{:S(2)}) collective-permute-start(f32[1,256]{1,0:T(1,128)S(1)} %add.3.mine_ref), channel_id=1, source_target_pairs={{0,3},{1,2},{2,1},{3,0},{4,7},{5,6},{6,5},{7,4},{8,11},{9,10},{10,... | collective-permute-start | bytes 3080 | tf_op jit(solution)/shard_map/ppermute | solution.py:310
  49.3 1.0 %copy.10 = bf16[256,2048]{1,0:T(8,128)(2,1)} copy(bf16[256,2048]{1,0:T(8,128)(2,1)S(1)} %get-tuple-element.76.new_ref) | data formatting | bytes 2097152
  50.2 0.4 collective-permute-done.7.other_ref
  50.7 0.0 copy-done
  50.7 1.3 %normalise.1 = bf16[256,2048]{1,0:T(8,128)(2,1)} custom-call(f32[1,256]{1,0:T(1,128)S(1)} %add.3.mine_ref, f32[1,256]{1,0:T(1,128)S(1)} %collective-permute-done.7.other_ref, f32[1,2048]{1,0:T(1,128)S(1)} %bitcast.2, bf16[256,2048]{1,0:T(8,128)(2,1)S(1)} %get-tuple-element.76.new_ref), custom_call_target="tpu_custom_call" | custom-call | tf_op jit(solution)/shard_map/normalise/pallas_call | solution.py:313
  (2 shorter events, 0.0 us)
Async XLA Ops:
  6.0 3.9 %collective-permute-start = (bf16[16,2048]{1,0:T(8,128)(2,1)S(1)}, bf16[16,2048]{1,0:T(8,128)(2,1)S(1)}, u32[]{:S(2)}, u32[]{:S(2)}) collective-permute-start(bf16[16,2048]{1,0:T(8,128)(2,1)S(1)} %get-tuple-element.39), channel_id=1, source_target_pairs={{0,4},{4,0},{8,12},{12,8},{16,20},{20,16},{24,28},{28,24},{32,36},... | collective-permute-start | bytes 196616 | tf_op jit(solution)/shard_map/ppermute | solution.py:287
  10.0 4.5 %collective-permute-start.1 = (bf16[16,2048]{1,0:T(8,128)(2,1)S(1)}, bf16[16,2048]{1,0:T(8,128)(2,1)S(1)}, u32[]{:S(2)}, u32[]{:S(2)}) collective-permute-start(bf16[16,2048]{1,0:T(8,128)(2,1)S(1)} %get-tuple-element.50), channel_id=1, source_target_pairs={{0,12},{4,8},{8,4},{12,0},{16,28},{20,24},{24,20},{28,16},{32,44},... | collective-permute-start | bytes 196616 | tf_op jit(solution)/shard_map/ppermute | solution.py:287
  14.5 3.2 %collective-permute-start.2 = (bf16[16,2048]{1,0:T(8,128)(2,1)S(1)}, bf16[16,2048]{1,0:T(8,128)(2,1)S(1)}, u32[]{:S(2)}, u32[]{:S(2)}) collective-permute-start(bf16[16,2048]{1,0:T(8,128)(2,1)S(1)} %get-tuple-element.55), channel_id=1, source_target_pairs={{0,16},{4,20},{8,24},{12,28},{16,0},{20,4},{24,8},{28,12},{32,48},... | collective-permute-start | bytes 196616 | tf_op jit(solution)/shard_map/ppermute | solution.py:287
  17.8 3.5 %collective-permute-start.3 = (bf16[16,2048]{1,0:T(8,128)(2,1)S(1)}, bf16[16,2048]{1,0:T(8,128)(2,1)S(1)}, u32[]{:S(2)}, u32[]{:S(2)}) collective-permute-start(bf16[16,2048]{1,0:T(8,128)(2,1)S(1)} %get-tuple-element.60), channel_id=1, source_target_pairs={{0,32},{4,36},{8,40},{12,44},{16,48},{20,52},{24,56},{28,60},{32,0... | collective-permute-start | bytes 196616 | tf_op jit(solution)/shard_map/ppermute | solution.py:287
  21.4 4.9 %collective-permute-start.4 = (bf16[16,2048]{1,0:T(8,128)(2,1)S(1)}, bf16[16,2048]{1,0:T(8,128)(2,1)S(1)}, u32[]{:S(2)}, u32[]{:S(2)}) collective-permute-start(bf16[16,2048]{1,0:T(8,128)(2,1)S(1)} %get-tuple-element.65), channel_id=1, source_target_pairs={{0,64},{4,68},{8,72},{12,76},{16,80},{20,84},{24,88},{28,92},{32,9... | collective-permute-start | bytes 196616 | tf_op jit(solution)/shard_map/ppermute | solution.py:287
  27.0 7.8 %collective-permute-start.5 = (bf16[16,2048]{1,0:T(8,128)(2,1)S(1)}, bf16[16,2048]{1,0:T(8,128)(2,1)S(1)}, u32[]{:S(2)}, u32[]{:S(2)}) collective-permute-start(bf16[16,2048]{1,0:T(8,128)(2,1)S(1)} %get-tuple-element.68), channel_id=1, source_target_pairs={{0,224},{4,228},{8,232},{12,236},{16,240},{20,244},{24,248},{28,25... | collective-permute-start | bytes 196616 | tf_op jit(solution)/shard_map/ppermute | solution.py:287
  34.9 15.8 %copy-start = (f32[2048]{0:T(1024)S(1)}, f32[2048]{0:T(1024)}, u32[]{:S(2)}) copy-start(f32[2048]{0:T(1024)} %param.15) | copy-start | bytes 24580
  38.1 8.0 %collective-permute-start.6 = (f32[1,256]{1,0:T(1,128)S(1)}, f32[1,256]{1,0:T(1,128)S(1)}, u32[]{:S(2)}, u32[]{:S(2)}) collective-permute-start(f32[1,256]{1,0:T(1,128)S(1)} %get-tuple-element.75), channel_id=1, source_target_pairs={{0,1},{1,0},{2,3},{3,2},{4,5},{5,4},{6,7},{7,6},{8,9},{9,8},{10,11... | collective-permute-start | bytes 3080 | tf_op jit(solution)/shard_map/ppermute | solution.py:309
  46.2 4.5 %collective-permute-start.7 = (f32[1,256]{1,0:T(1,128)S(1)}, f32[1,256]{1,0:T(1,128)S(1)}, u32[]{:S(2)}, u32[]{:S(2)}) collective-permute-start(f32[1,256]{1,0:T(1,128)S(1)} %add.3.mine_ref), channel_id=1, source_target_pairs={{0,3},{1,2},{2,1},{3,0},{4,7},{5,6},{6,5},{7,4},{8,11},{9,10},{10,... | collective-permute-start | bytes 3080 | tf_op jit(solution)/shard_map/ppermute | solution.py:310
where the time goes:
time: 52.1 us; the launch traced here: 52 us
  starting transfers between devices  27 us (52%)
  Pallas kernels  18 us (35%)
  waiting for transfers between devices  5.22 us (10%)
  local copies, waits for them, and re-layouts  0.98 us (2%)
  between operations  0.75 us (1%)
    ppermute x6, starting transfers between devices, shards(): arrived = lax.ppermute(sent, 'ctx', pairs)  16.7 us
    ppermute x1, starting transfers between devices, shards(): power = power + lax.ppermute(power, 'tp', [(i, i ^ 1) for i in range(4)])  7.2 us
    pallas_call x4, Pallas kernels, local_piece(): pl.pallas_call(functools.partial(local_kernel, span, piece), in_specs=[in...  7.05 us
    pallas_call x1, Pallas kernels, shards(): pl.pallas_call(functools.partial(state_kernel, span), in_specs=[anywhere]...  5.33 us
    ppermute x6, waiting for transfers between devices, shards(): arrived = lax.ppermute(sent, 'ctx', pairs)  3.99 us
    pallas_call x1, Pallas kernels, shards(): pl.pallas_call(finish_kernel, in_specs=[in_vmem] * (4 + pieces), out_spec...  3.24 us
    ppermute x1, starting transfers between devices, shards(): other = lax.ppermute(power, 'tp', [(i, i ^ 3) for i in range(4)])  3.12 us
    pallas_call x1, Pallas kernels, shards(): pl.pallas_call(functools.partial(norm_kernel, channels), in_specs=[in_vme...  1.31 us
  transfers between devices with their start and end apart: 8, of which 4 were waited for; matrix products, arithmetic and copies ran while one was open for 2% of the time, Pallas kernels for 14%

commit v1 on v0

v1 whole, which is shorter than its diff:
```python
import functools

import jax
import jax.numpy as jnp
from jax import lax
from jax.experimental import pallas as pl
from jax.experimental.pallas import tpu as pltpu
from jax.sharding import PartitionSpec as P

epsilon = 1e-06
lanes = 128
sublanes = 8
piece_width = 512
vmem_bytes = 24 * 1024 * 1024


def at_group(group):
    return pl.ds(pl.multiple_of(group * lanes, lanes), lanes)


def spread(ref, mode, cols):
    return jnp.broadcast_to(ref[pl.ds(mode, 1), cols], (sublanes, lanes))


def tree_sum(parts):
    parts = list(parts)
    while len(parts) > 1:
        parts = [l + r for l, r in zip(parts[::2], parts[1::2])]
    return parts[0]


def state_kernel(
    q_hbm, k_hbm, v_hbm, x_hbm, decay_hbm, res_hbm, skip_hbm,
    total_ref, sent_ref, sig_ref, v_ref, x_ref, decay_ref, res_ref, skip_ref, tile_ref,
    q_ref, k_ref, over_ref, pair_sem, side_sem,
):
    modes = decay_ref.shape[0]
    rows, width = q_ref.shape
    edges = [0, 256, 512] + list(range(1024, width + 1, 512))
    pair = []
    first = pltpu.make_async_copy(decay_hbm, decay_ref, side_sem.at[0])
    first.start()
    for p, (low, high) in enumerate(zip(edges, edges[1:])):
        cols = pl.ds(low, high - low)
        for at, (src, dst) in enumerate(((q_hbm, q_ref), (k_hbm, k_ref))):
            pair.append(pltpu.make_async_copy(src.at[:, cols], dst.at[:, cols], pair_sem.at[at, p]))
            pair[-1].start()
    side = []
    for at, (src, dst) in enumerate(((res_hbm, res_ref), (skip_hbm, skip_ref), (v_hbm, v_ref), (x_hbm, x_ref))):
        side.append(pltpu.make_async_copy(src, dst, side_sem.at[at + 1]))
        side[-1].start()
    first.wait()
    decay = decay_ref[...]
    tile_ref[...] = jnp.exp(decay * float(-sublanes))
    for at in range(3):
        over_ref[pl.ds(at * modes, modes), :] = jnp.exp(decay * float(-1 << at))
    for p, (low, high) in enumerate(zip(edges, edges[1:])):
        pair[2 * p].wait()
        pair[2 * p + 1].wait()

        @pl.loop(low // lanes, high // lanes)
        def _(group):
            cols = at_group(group)
            steps = [spread(tile_ref, n, cols) for n in range(modes)]
            states = None
            for j in range(0, rows, 2 * sublanes):
                at = pl.ds(j, 2 * sublanes)
                sig = q_ref[at, cols] * k_ref[at, cols]
                sig_ref[at, cols] = sig
                sig = sig.astype(jnp.float32)
                for part in (sig[:sublanes], sig[sublanes:]):
                    states = [s * a + part for s, a in zip(states, steps)] if states else [part] * modes
            for n in range(modes):
                state = states[n]
                for at in range(3):
                    state = state + spread(over_ref, at * modes + n, cols) * pltpu.roll(state, 1 << at, 0)
                total_ref[pl.ds(n, 1), cols] = state[sublanes - 1 :]
            sent_ref[:, cols] = total_ref[:, cols].astype(jnp.bfloat16)

    for copy in side:
        copy.wait()


def local_kernel(
    piece, decay_ref, res_ref, skip_ref, sig_ref, v_ref, x_ref, base_ref, lead_ref, rows_ref, runs_ref, conv_ref
):
    modes = decay_ref.shape[0]
    span = sig_ref.shape[0] // sublanes
    run = lax.broadcasted_iota(jnp.int32, (sublanes, lanes), 0)
    ahead = (run + 1).astype(jnp.float32)

    def shifted(state, by):
        return jnp.where(run >= by, pltpu.roll(state, by, 0), 0.0)

    @pl.loop(0, piece_width // lanes)
    def _(group):
        here = at_group(group)
        cols = at_group(group + piece * (piece_width // lanes))
        rows_ref[...] = sig_ref[:, cols].astype(jnp.float32)
        for j in range(span):
            runs_ref[pl.ds(j * sublanes, sublanes), :] = rows_ref[pl.ds(j, sublanes, stride=span), :]
        skip = jnp.broadcast_to(skip_ref[:, cols], (sublanes, lanes))
        half = modes // 2
        for low in range(0, modes, half):
            decays = [spread(decay_ref, n, cols) for n in range(low, low + half)]
            gains = [spread(res_ref, n, cols) for n in range(low, low + half)]
            steps = [jnp.exp(-d) for d in decays]
            states = None
            for j in range(span):
                sig = runs_ref[pl.ds(j * sublanes, sublanes), :]
                states = [s * a + sig for s, a in zip(states, steps)] if j else [sig] * half
            for n in range(half):
                state = states[n]
                over = jnp.exp(decays[n] * float(-span))
                for by in (1, 2, 4):
                    state = state + over * shifted(state, by)
                    over = over * over
                states[n] = gains[n] * shifted(state, 1)
                lead_ref[low + n, :, here] = gains[n] * jnp.exp(-decays[n] * ahead)
            for j in range(span):
                sig = runs_ref[pl.ds(j * sublanes, sublanes), :]
                states = [s * a + sig * g for s, a, g in zip(states, steps, gains)]
                out = conv_ref.at[pl.ds(j, sublanes, stride=span), :]
                if low == 0:
                    out[...] = tree_sum(states) + skip * sig
                else:
                    out[...] = out[...] + tree_sum(states)
        mixed = v_ref[:, cols].astype(jnp.float32) * conv_ref[...]
        base_ref[:, here] = x_ref[:, cols].astype(jnp.float32) + mixed


def merge_kernel(size, rows, last, arrived_ref, decay_ref, *rest):
    if size == 1:
        total_ref, rest = rest[0], rest[1:]
    elif last:
        enter_ref, rest = rest[0], rest[1:]
    else:
        total_ref, enter_ref, rest = rest[0], rest[1], rest[2:]
    position = lax.axis_index("ctx")
    arrived = arrived_ref[...].astype(jnp.float32)
    decay = decay_ref[...]
    upper = (position & size) != 0
    within = (position & (size - 1)).astype(jnp.float32) * float(rows)
    share = jnp.where(upper, arrived, 0.0) * jnp.exp(decay * -within)
    rest[0][...] = share if size == 1 else enter_ref[...] + share
    if not last:
        over = jnp.exp(decay * float(-rows * size))
        total = total_ref[...]
        total = jnp.where(upper, total + over * arrived, over * total + arrived)
        rest[1][...] = total.astype(jnp.bfloat16)
        if len(rest) > 2:
            rest[2][...] = total


def finish_kernel(enter_ref, tile_ref, v_ref, *rest):
    pieces = (len(rest) - 3) // 2
    base_refs, lead_refs = rest[:pieces], rest[pieces:-3]
    new_ref, power_ref, acc_ref = rest[-3:]
    modes = tile_ref.shape[0]
    rows = v_ref.shape[0]
    acc_ref[...] = jnp.zeros_like(acc_ref)
    for piece, (base_ref, lead_ref) in enumerate(zip(base_refs, lead_refs)):

        @pl.loop(0, piece_width // lanes)
        def _(group):
            here = at_group(group)
            cols = at_group(group + piece * (piece_width // lanes))
            steps = [spread(tile_ref, n, cols) for n in range(modes)]
            states = [lead_ref[n, :, here] * spread(enter_ref, n, cols) for n in range(modes)]
            for pair in range(rows // (2 * sublanes)):
                halves = []
                for half in range(2):
                    halves.append(tree_sum(states))
                    states = [s * a for s, a in zip(states, steps)]
                at = pl.ds(pair * 2 * sublanes, 2 * sublanes)
                carried = jnp.concatenate(halves, axis=0)
                fresh = base_ref[at, here] + v_ref[at, cols].astype(jnp.float32) * carried
                fresh = fresh.astype(jnp.bfloat16)
                new_ref[at, cols] = fresh
                fresh = fresh.astype(jnp.float32)
                acc_ref[at, :] += fresh * fresh

    ones = jnp.ones((sublanes, lanes), jnp.float32)
    sums = lax.dot_general(
        ones,
        acc_ref[...],
        (((1,), (1,)), ((), ())),
        precision=lax.Precision.HIGHEST,
        preferred_element_type=jnp.float32,
    )
    power_ref[...] = sums[0:1]


def norm_kernel(channels, mine_ref, other_ref, gain_ref, new_ref, out_hbm, inv_ref, out_ref, sem):
    rows, width = new_ref.shape
    power = (mine_ref[...] + other_ref[...]) * (1.0 / channels)
    inverse = lax.rsqrt(power + epsilon)
    inv_ref[...] = jnp.transpose(jnp.broadcast_to(inverse, (lanes, rows)))
    copies = []
    part = width // sem.shape[0]
    for p in range(sem.shape[0]):

        @pl.loop(p * part // lanes, (p + 1) * part // lanes)
        def _(group):
            cols = at_group(group)
            scaled = new_ref[:, cols].astype(jnp.float32) * inv_ref[...] * gain_ref[:, cols]
            out_ref[:, cols] = scaled.astype(jnp.bfloat16)

        cols = pl.ds(p * part, part)
        copies.append(pltpu.make_async_copy(out_ref.at[:, cols], out_hbm.at[:, cols], sem.at[p]))
        copies[-1].start()
    for copy in copies:
        copy.wait()


def shards(queries, key_proj, values, residues, decay_rates, skip_weight, stream, norm_gain):
    rows, width = queries.shape
    modes = decay_rates.shape[0]
    params = pltpu.CompilerParams(vmem_limit_bytes=vmem_bytes)
    f32, bf16 = jnp.float32, jnp.bfloat16
    in_vmem = pl.BlockSpec(memory_space=pltpu.VMEM)
    anywhere = pl.BlockSpec(memory_space=pl.ANY)
    pieces = width // piece_width

    far = [queries, key_proj, values, stream, decay_rates, residues, skip_weight[None, :]]
    far = [pltpu.with_memory_space_constraint(a, pltpu.HBM) for a in far]
    outs = [
        ((modes, width), f32),
        ((modes, width), bf16),
        ((rows, width), bf16),
        ((rows, width), bf16),
        ((rows, width), bf16),
        ((modes, width), f32),
        ((modes, width), f32),
        ((1, width), f32),
        ((modes, width), f32),
    ]
    total, sent, signal, near_values, near_stream, decay, gains, skip, tile = pl.pallas_call(
        state_kernel,
        in_specs=[anywhere] * len(far),
        out_specs=[in_vmem] * len(outs),
        out_shape=[pltpu.VMEM(shape, dtype) for shape, dtype in outs],
        scratch_shapes=[
            pltpu.VMEM((rows, width), bf16),
            pltpu.VMEM((rows, width), bf16),
            pltpu.VMEM((3 * modes, width), f32),
            pltpu.SemaphoreType.DMA((2, pieces + 1)),
            pltpu.SemaphoreType.DMA((5,)),
        ],
        compiler_params=params,
        cost_estimate=pl.CostEstimate(flops=2 * modes * rows * width, bytes_accessed=4 * rows * width, transcendentals=0),
        name="states",
    )(*far)

    def local_piece(piece, decay):
        return pl.pallas_call(
            functools.partial(local_kernel, piece),
            in_specs=[in_vmem] * 6,
            out_specs=[in_vmem] * 2,
            out_shape=[pltpu.VMEM((rows, piece_width), f32), pltpu.VMEM((modes, sublanes, piece_width), f32)],
            scratch_shapes=[pltpu.VMEM((rows, lanes), f32)] * 3,
            compiler_params=params,
            cost_estimate=pl.CostEstimate(
                flops=6 * modes * rows * piece_width, bytes_accessed=12 * rows * piece_width, transcendentals=0
            ),
            name="local",
        )(decay, gains, skip, signal, near_values, near_stream)

    def link(partner_of):
        places = [(z, y, x) for z in range(8) for y in range(2) for x in range(4)]
        index = lambda z, y, x: (z * 2 + y) * 4 + x
        return [(index(*at), index(*partner_of(*at))) for at in places]

    rounds = [
        link(lambda z, y, x: (z, y, x ^ 1)),
        link(lambda z, y, x: (z, y, x ^ 3)),
        link(lambda z, y, x: (z, y ^ 1, x)),
        link(lambda z, y, x: (z ^ 1, y, x)),
        link(lambda z, y, x: (z ^ 2, y, x)),
        link(lambda z, y, x: ((6, 7, 4, 5, 2, 3, 0, 1)[z], y, x)),
    ]
    def merge(size, last, keep, arrived, total, enter):
        operands = [arrived, decay] + ([] if last else [total]) + ([] if size == 1 else [enter])
        outs = [f32] if last else [f32, bf16, f32] if keep else [f32, bf16]
        return pl.pallas_call(
            functools.partial(merge_kernel, size, rows, last),
            in_specs=[in_vmem] * len(operands),
            out_specs=[in_vmem] * len(outs),
            out_shape=[pltpu.VMEM((modes, width), dtype) for dtype in outs],
            compiler_params=params,
            name="merge",
        )(*operands)

    enter = None
    bases, leads = [], []
    for level, pairs in enumerate(rounds):
        arrived = lax.ppermute(sent, "ctx", pairs)
        if level < pieces:
            tied, sent = lax.optimization_barrier((decay, sent))
            base, lead = local_piece(level, tied)
            arrived, base = lax.optimization_barrier((arrived, base))
            bases.append(base)
            leads.append(lead)
        last = level + 1 == len(rounds)
        keep = level + 2 < len(rounds)
        merged = merge(1 << level, last, keep, arrived, total, enter)
        enter = merged[0]
        if not last:
            sent = merged[1]
        if keep:
            total = merged[2]

    fresh, power = pl.pallas_call(
        finish_kernel,
        in_specs=[in_vmem] * (3 + 2 * pieces),
        out_specs=[in_vmem] * 2,
        out_shape=[pltpu.VMEM((rows, width), bf16), pltpu.VMEM((1, rows), f32)],
        scratch_shapes=[pltpu.VMEM((rows, lanes), f32)],
        compiler_params=params,
        cost_estimate=pl.CostEstimate(flops=2 * modes * rows * width, bytes_accessed=8 * rows * width, transcendentals=0),
        name="finish",
    )(enter, tile, near_values, *bases, *leads)

    power = power + lax.ppermute(power, "tp", [(i, i ^ 1) for i in range(4)])
    other = lax.ppermute(power, "tp", [(i, i ^ 3) for i in range(4)])

    channels = width * lax.axis_size("tp")
    normed = pl.pallas_call(
        functools.partial(norm_kernel, channels),
        in_specs=[in_vmem] * 4,
        out_specs=anywhere,
        out_shape=pltpu.HBM((rows, width), bf16),
        scratch_shapes=[
            pltpu.VMEM((rows, lanes), f32),
            pltpu.VMEM((rows, width), bf16),
            pltpu.SemaphoreType.DMA((8,)),
        ],
        compiler_params=params,
        name="normalise",
    )(power, other, norm_gain[None, :], fresh)
    return (fresh, normed)


def solution(mesh):
    in_specs = (
        P("ctx", "tp"),
        P("ctx", "tp"),
        P("ctx", "tp"),
        P(None, "tp"),
        P(None, "tp"),
        P("tp"),
        P("ctx", "tp"),
        P("tp"),
    )
    out_specs = (P("ctx", "tp"), P("ctx", "tp"))
    return jax.shard_map(shards, mesh=mesh, in_specs=in_specs, out_specs=out_specs, check_vma=False)
```

time: 52.1 us -> 49.5 us (0.950)
  starting transfers between devices: 27 us -> 22.4 us
  Pallas kernels: 18 us -> 19.8 us
    ppermute x6, starting transfers between devices: 16.7 us -> 14.2 us  [shards(): arrived = lax.ppermute(sent, 'ctx', pairs)]
    pallas_call x6, Pallas kernels: 15.6 us -> 18 us  [the longest x4 10.7 us: local_piece(): pl.pallas_call(functools.partial(local_kernel, piece), in_specs=[in_vmem]...]
    ppermute x1, starting transfers between devices: 7.2 us -> 5.31 us  [shards(): power = power + lax.ppermute(power, 'tp', [(i, i ^ 1) for i in range(4)])]
    pallas_call x6, Pallas kernels: 1.06 us -> 0.41 us  [merge(): pl.pallas_call(functools.partial(merge_kernel, size, rows, last), in_spec...]
  transfers between devices with their start and end apart: 8 -> 8, of which waited for: 4 -> 4; matrix products, arithmetic and copies ran while one was open for 2% -> 2% of each run, Pallas kernels for 14% -> 22%
where the time goes in v1:
time: 49.5 us; the launch traced here: 49.4 us
  starting transfers between devices  22.4 us (45%)
  Pallas kernels  19.8 us (40%)
  waiting for transfers between devices  5.48 us (11%)
  local copies, waits for them, and re-layouts  0.97 us (2%)
  between operations  0.74 us (1%)
    ppermute x6, starting transfers between devices, shards(): arrived = lax.ppermute(sent, 'ctx', pairs)  14.2 us
    pallas_call x4, Pallas kernels, local_piece(): pl.pallas_call(functools.partial(local_kernel, piece), in_specs=[in_vmem]...  10.7 us
    ppermute x1, starting transfers between devices, shards(): power = power + lax.ppermute(power, 'tp', [(i, i ^ 1) for i in range(4)])  5.31 us
    pallas_call x1, Pallas kernels, shards(): pl.pallas_call(state_kernel, in_specs=[anywhere] * len(far), out_specs=[i...  4.29 us
    ppermute x6, waiting for transfers between devices, shards(): arrived = lax.ppermute(sent, 'ctx', pairs)  4.08 us
    pallas_call x1, Pallas kernels, shards(): pl.pallas_call(finish_kernel, in_specs=[in_vmem] * (3 + 2 * pieces), out_...  3.05 us
    ppermute x1, starting transfers between devices, shards(): other = lax.ppermute(power, 'tp', [(i, i ^ 3) for i in range(4)])  2.94 us
    pallas_call x1, Pallas kernels, shards(): pl.pallas_call(functools.partial(norm_kernel, channels), in_specs=[in_vme...  1.31 us
  transfers between devices with their start and end apart: 8, of which 4 were waited for; matrix products, arithmetic and copies ran while one was open for 2% of the time, Pallas kernels for 22%

profile of v1, /device:TPU:1, one launch (start us, length us, event | category | flops | bytes accessed | tf_op | source)
XLA Modules:
  0.0 49.4 jit_solution(16616293166261472787)
XLA Ops:
  0.6 4.3 %states.1 = (f32[16,2048]{1,0:T(8,128)S(1)}, bf16[16,2048]{1,0:T(8,128)(2,1)S(1)}, bf16[256,2048]{1,0:T(8,128)(2,1)S(1)}, bf16[256,2048]{1,0:T(8,128)(2,1)S(1)},...) custom-call(bf16[256,2048]{1,0:T(8,128)(2,1)} %q_hbm.1, ...), custom_call_target="tpu_custom_call" | custom-call | flops 16777216 | bytes 2097152 | tf_op jit(solution)/shard_map/states/pallas_call | solution.py:238
  4.9 2.1 %collective-permute-start = (bf16[16,2048]{1,0:T(8,128)(2,1)S(1)}, bf16[16,2048]{1,0:T(8,128)(2,1)S(1)}, u32[]{:S(2)}, u32[]{:S(2)}) collective-permute-start(bf16[16,2048]{1,0:T(8,128)(2,1)S(1)} %get-tuple-element.47), channel_id=1, source_target_pairs={{0,4},{4,0},{8,12},{12,8},{16,20},{20,16},{24,28},{28,24},{32,36},... | collective-permute-start | bytes 196616 | tf_op jit(solution)/shard_map/ppermute | solution.py:297
  7.1 2.7 %local.4 = (f32[256,512]{1,0:T(8,128)S(1)}, f32[16,8,512]{2,1,0:T(8,128)S(1)}) custom-call(f32[16,2048]{1,0:T(8,128)S(1)} %get-tuple-element.71.decay_ref, f32[16,2048]{1,0:T(8,128)S(1)} %get-tuple-element.50.res_ref, f32[1,2048]{1,0:T(1,128)S(1)} %get-tuple-element.51.skip_ref, bf16[256,2048]{1,0:T(8,128)(2,1)S(1)} %get-tuple-element.52.sig_ref, ...), custom_call_target="tpu_custom_call" | custom-call | flops 12582912 | bytes 1572864 | tf_op jit(solution)/shard_map/local/pallas_call | solution.py:256
  9.8 0.0 collective-permute-done.arrived_ref
  9.8 0.1 merge.6
  9.8 1.9 %collective-permute-start.1 = (bf16[16,2048]{1,0:T(8,128)(2,1)S(1)}, bf16[16,2048]{1,0:T(8,128)(2,1)S(1)}, u32[]{:S(2)}, u32[]{:S(2)}) collective-permute-start(bf16[16,2048]{1,0:T(8,128)(2,1)S(1)} %get-tuple-element.58), channel_id=1, source_target_pairs={{0,12},{4,8},{8,4},{12,0},{16,28},{20,24},{24,20},{28,16},{32,44},... | collective-permute-start | bytes 196616 | tf_op jit(solution)/shard_map/ppermute | solution.py:297
  11.7 2.7 %local.5 = (f32[256,512]{1,0:T(8,128)S(1)}, f32[16,8,512]{2,1,0:T(8,128)S(1)}) custom-call(f32[16,2048]{1,0:T(8,128)S(1)} %get-tuple-element.71.decay_ref, f32[16,2048]{1,0:T(8,128)S(1)} %get-tuple-element.50.res_ref, f32[1,2048]{1,0:T(1,128)S(1)} %get-tuple-element.51.skip_ref, bf16[256,2048]{1,0:T(8,128)(2,1)S(1)} %get-tuple-element.52.sig_ref, ...), custom_call_target="tpu_custom_call" | custom-call | flops 12582912 | bytes 1572864 | tf_op jit(solution)/shard_map/local/pallas_call | solution.py:256
  14.4 0.0 collective-permute-done.1.arrived_ref
  14.4 0.1 merge.7
  14.5 1.4 %collective-permute-start.2 = (bf16[16,2048]{1,0:T(8,128)(2,1)S(1)}, bf16[16,2048]{1,0:T(8,128)(2,1)S(1)}, u32[]{:S(2)}, u32[]{:S(2)}) collective-permute-start(bf16[16,2048]{1,0:T(8,128)(2,1)S(1)} %get-tuple-element.64), channel_id=1, source_target_pairs={{0,16},{4,20},{8,24},{12,28},{16,0},{20,4},{24,8},{28,12},{32,48},... | collective-permute-start | bytes 196616 | tf_op jit(solution)/shard_map/ppermute | solution.py:297
  15.9 2.7 %local.6 = (f32[256,512]{1,0:T(8,128)S(1)}, f32[16,8,512]{2,1,0:T(8,128)S(1)}) custom-call(f32[16,2048]{1,0:T(8,128)S(1)} %get-tuple-element.71.decay_ref, f32[16,2048]{1,0:T(8,128)S(1)} %get-tuple-element.50.res_ref, f32[1,2048]{1,0:T(1,128)S(1)} %get-tuple-element.51.skip_ref, bf16[256,2048]{1,0:T(8,128)(2,1)S(1)} %get-tuple-element.52.sig_ref, ...), custom_call_target="tpu_custom_call" | custom-call | flops 12582912 | bytes 1572864 | tf_op jit(solution)/shard_map/local/pallas_call | solution.py:256
  18.6 0.0 collective-permute-done.2.arrived_ref
  18.6 0.1 merge.8
  18.7 1.7 %collective-permute-start.3 = (bf16[16,2048]{1,0:T(8,128)(2,1)S(1)}, bf16[16,2048]{1,0:T(8,128)(2,1)S(1)}, u32[]{:S(2)}, u32[]{:S(2)}) collective-permute-start(bf16[16,2048]{1,0:T(8,128)(2,1)S(1)} %get-tuple-element.70), channel_id=1, source_target_pairs={{0,32},{4,36},{8,40},{12,44},{16,48},{20,52},{24,56},{28,60},{32,0... | collective-permute-start | bytes 196616 | tf_op jit(solution)/shard_map/ppermute | solution.py:297
  20.4 2.7 %local.7 = (f32[256,512]{1,0:T(8,128)S(1)}, f32[16,8,512]{2,1,0:T(8,128)S(1)}) custom-call(f32[16,2048]{1,0:T(8,128)S(1)} %get-tuple-element.71.decay_ref, f32[16,2048]{1,0:T(8,128)S(1)} %get-tuple-element.50.res_ref, f32[1,2048]{1,0:T(1,128)S(1)} %get-tuple-element.51.skip_ref, bf16[256,2048]{1,0:T(8,128)(2,1)S(1)} %get-tuple-element.52.sig_ref, ...), custom_call_target="tpu_custom_call" | custom-call | flops 12582912 | bytes 1572864 | tf_op jit(solution)/shard_map/local/pallas_call | solution.py:256
  23.1 0.0 collective-permute-done.3.arrived_ref
  23.1 0.1 merge.9
  23.2 3.1 %collective-permute-start.4 = (bf16[16,2048]{1,0:T(8,128)(2,1)S(1)}, bf16[16,2048]{1,0:T(8,128)(2,1)S(1)}, u32[]{:S(2)}, u32[]{:S(2)}) collective-permute-start(bf16[16,2048]{1,0:T(8,128)(2,1)S(1)} %get-tuple-element.76), channel_id=1, source_target_pairs={{0,64},{4,68},{8,72},{12,76},{16,80},{20,84},{24,88},{28,92},{32,9... | collective-permute-start | bytes 196616 | tf_op jit(solution)/shard_map/ppermute | solution.py:297
  26.2 2.4 %collective-permute-done.4.arrived_ref = bf16[16,2048]{1,0:T(8,128)(2,1)S(1)} collective-permute-done((bf16[16,2048]{1,0:T(8,128)(2,1)S(1)}, bf16[16,2048]{1,0:T(8,128)(2,1)S(1)}, u32[]{:S(2)}, u32[]{:S(2)}) %collective-permute-start.4) | collective-permute-done | bytes 65568 | tf_op jit(solution)/shard_map/ppermute | solution.py:297
  28.6 0.1 merge.10
  28.7 4.0 %collective-permute-start.5 = (bf16[16,2048]{1,0:T(8,128)(2,1)S(1)}, bf16[16,2048]{1,0:T(8,128)(2,1)S(1)}, u32[]{:S(2)}, u32[]{:S(2)}) collective-permute-start(bf16[16,2048]{1,0:T(8,128)(2,1)S(1)} %get-tuple-element.79), channel_id=1, source_target_pairs={{0,192},{4,196},{8,200},{12,204},{16,208},{20,212},{24,216},{28,22... | collective-permute-start | bytes 196616 | tf_op jit(solution)/shard_map/ppermute | solution.py:297
  32.7 1.7 %collective-permute-done.5.arrived_ref = bf16[16,2048]{1,0:T(8,128)(2,1)S(1)} collective-permute-done((bf16[16,2048]{1,0:T(8,128)(2,1)S(1)}, bf16[16,2048]{1,0:T(8,128)(2,1)S(1)}, u32[]{:S(2)}, u32[]{:S(2)}) %collective-permute-start.5) | collective-permute-done | bytes 65568 | tf_op jit(solution)/shard_map/ppermute | solution.py:297
  34.4 3.1 %finish.1 = (bf16[256,2048]{1,0:T(8,128)(2,1)S(1)}, f32[1,256]{1,0:T(1,128)S(1)}) custom-call(f32[16,2048]{1,0:T(8,128)S(1)} %merge.11.enter_ref, f32[16,2048]{1,0:T(8,128)S(1)} %get-tuple-element.81.tile_ref, bf16[256,2048]{1,0:T(8,128)(2,1)S(1)} %get-tuple-element.53.v_ref, f32[256,512]{1,0:T(8,128)S(1)} %get-tuple-element.82.rest_0_, ...), custom_call_target="tpu_custom_call" | custom-call | flops 16777216 | bytes 4194304 | tf_op jit(solution)/shard_map/finish/pallas_call | solution.py:313
  37.5 5.3 %collective-permute-start.6 = (f32[1,256]{1,0:T(1,128)S(1)}, f32[1,256]{1,0:T(1,128)S(1)}, u32[]{:S(2)}, u32[]{:S(2)}) collective-permute-start(f32[1,256]{1,0:T(1,128)S(1)} %get-tuple-element.91), channel_id=1, source_target_pairs={{0,1},{1,0},{2,3},{3,2},{4,5},{5,4},{6,7},{7,6},{8,9},{9,8},{10,11... | collective-permute-start | bytes 3080 | tf_op jit(solution)/shard_map/ppermute | solution.py:324
  42.8 0.8 %collective-permute-done.6 = f32[1,256]{1,0:T(1,128)S(1)} collective-permute-done((f32[1,256]{1,0:T(1,128)S(1)}, f32[1,256]{1,0:T(1,128)S(1)}, u32[]{:S(2)}, u32[]{:S(2)}) %collective-permute-start.6) | collective-permute-done | bytes 1056 | tf_op jit(solution)/shard_map/ppermute | solution.py:324
  43.6 2.9 %collective-permute-start.7 = (f32[1,256]{1,0:T(1,128)S(1)}, f32[1,256]{1,0:T(1,128)S(1)}, u32[]{:S(2)}, u32[]{:S(2)}) collective-permute-start(f32[1,256]{1,0:T(1,128)S(1)} %add.3.mine_ref), channel_id=1, source_target_pairs={{0,3},{1,2},{2,1},{3,0},{4,7},{5,6},{6,5},{7,4},{8,11},{9,10},{10,... | collective-permute-start | bytes 3080 | tf_op jit(solution)/shard_map/ppermute | solution.py:325
  46.5 0.0 copy-start
  46.5 1.0 %copy.10 = bf16[256,2048]{1,0:T(8,128)(2,1)} copy(bf16[256,2048]{1,0:T(8,128)(2,1)S(1)} %get-tuple-element.92.new_ref) | data formatting | bytes 2097152
  47.5 0.6 %collective-permute-done.7.other_ref = f32[1,256]{1,0:T(1,128)S(1)} collective-permute-done((f32[1,256]{1,0:T(1,128)S(1)}, f32[1,256]{1,0:T(1,128)S(1)}, u32[]{:S(2)}, u32[]{:S(2)}) %collective-permute-start.7) | collective-permute-done | bytes 1056 | tf_op jit(solution)/shard_map/ppermute | solution.py:325
  48.1 0.0 copy-done
  48.1 1.3 %normalise.1 = bf16[256,2048]{1,0:T(8,128)(2,1)} custom-call(f32[1,256]{1,0:T(1,128)S(1)} %add.3.mine_ref, f32[1,256]{1,0:T(1,128)S(1)} %collective-permute-done.7.other_ref, f32[1,2048]{1,0:T(1,128)S(1)} %bitcast.2, bf16[256,2048]{1,0:T(8,128)(2,1)S(1)} %get-tuple-element.92.new_ref), custom_call_target="tpu_custom_call" | custom-call | tf_op jit(solution)/shard_map/normalise/pallas_call | solution.py:328
  (2 shorter events, 0.0 us)
Async XLA Ops:
  4.9 4.8 %collective-permute-start = (bf16[16,2048]{1,0:T(8,128)(2,1)S(1)}, bf16[16,2048]{1,0:T(8,128)(2,1)S(1)}, u32[]{:S(2)}, u32[]{:S(2)}) collective-permute-start(bf16[16,2048]{1,0:T(8,128)(2,1)S(1)} %get-tuple-element.47), channel_id=1, source_target_pairs={{0,4},{4,0},{8,12},{12,8},{16,20},{20,16},{24,28},{28,24},{32,36},... | collective-permute-start | bytes 196616 | tf_op jit(solution)/shard_map/ppermute | solution.py:297
  9.8 4.6 %collective-permute-start.1 = (bf16[16,2048]{1,0:T(8,128)(2,1)S(1)}, bf16[16,2048]{1,0:T(8,128)(2,1)S(1)}, u32[]{:S(2)}, u32[]{:S(2)}) collective-permute-start(bf16[16,2048]{1,0:T(8,128)(2,1)S(1)} %get-tuple-element.58), channel_id=1, source_target_pairs={{0,12},{4,8},{8,4},{12,0},{16,28},{20,24},{24,20},{28,16},{32,44},... | collective-permute-start | bytes 196616 | tf_op jit(solution)/shard_map/ppermute | solution.py:297
  14.5 4.1 %collective-permute-start.2 = (bf16[16,2048]{1,0:T(8,128)(2,1)S(1)}, bf16[16,2048]{1,0:T(8,128)(2,1)S(1)}, u32[]{:S(2)}, u32[]{:S(2)}) collective-permute-start(bf16[16,2048]{1,0:T(8,128)(2,1)S(1)} %get-tuple-element.64), channel_id=1, source_target_pairs={{0,16},{4,20},{8,24},{12,28},{16,0},{20,4},{24,8},{28,12},{32,48},... | collective-permute-start | bytes 196616 | tf_op jit(solution)/shard_map/ppermute | solution.py:297
  18.7 4.4 %collective-permute-start.3 = (bf16[16,2048]{1,0:T(8,128)(2,1)S(1)}, bf16[16,2048]{1,0:T(8,128)(2,1)S(1)}, u32[]{:S(2)}, u32[]{:S(2)}) collective-permute-start(bf16[16,2048]{1,0:T(8,128)(2,1)S(1)} %get-tuple-element.70), channel_id=1, source_target_pairs={{0,32},{4,36},{8,40},{12,44},{16,48},{20,52},{24,56},{28,60},{32,0... | collective-permute-start | bytes 196616 | tf_op jit(solution)/shard_map/ppermute | solution.py:297
  23.2 5.4 %collective-permute-start.4 = (bf16[16,2048]{1,0:T(8,128)(2,1)S(1)}, bf16[16,2048]{1,0:T(8,128)(2,1)S(1)}, u32[]{:S(2)}, u32[]{:S(2)}) collective-permute-start(bf16[16,2048]{1,0:T(8,128)(2,1)S(1)} %get-tuple-element.76), channel_id=1, source_target_pairs={{0,64},{4,68},{8,72},{12,76},{16,80},{20,84},{24,88},{28,92},{32,9... | collective-permute-start | bytes 196616 | tf_op jit(solution)/shard_map/ppermute | solution.py:297
  28.7 5.7 %collective-permute-start.5 = (bf16[16,2048]{1,0:T(8,128)(2,1)S(1)}, bf16[16,2048]{1,0:T(8,128)(2,1)S(1)}, u32[]{:S(2)}, u32[]{:S(2)}) collective-permute-start(bf16[16,2048]{1,0:T(8,128)(2,1)S(1)} %get-tuple-element.79), channel_id=1, source_target_pairs={{0,192},{4,196},{8,200},{12,204},{16,208},{20,212},{24,216},{28,22... | collective-permute-start | bytes 196616 | tf_op jit(solution)/shard_map/ppermute | solution.py:297
  37.5 6.1 %collective-permute-start.6 = (f32[1,256]{1,0:T(1,128)S(1)}, f32[1,256]{1,0:T(1,128)S(1)}, u32[]{:S(2)}, u32[]{:S(2)}) collective-permute-start(f32[1,256]{1,0:T(1,128)S(1)} %get-tuple-element.91), channel_id=1, source_target_pairs={{0,1},{1,0},{2,3},{3,2},{4,5},{5,4},{6,7},{7,6},{8,9},{9,8},{10,11... | collective-permute-start | bytes 3080 | tf_op jit(solution)/shard_map/ppermute | solution.py:324
  43.6 4.5 %collective-permute-start.7 = (f32[1,256]{1,0:T(1,128)S(1)}, f32[1,256]{1,0:T(1,128)S(1)}, u32[]{:S(2)}, u32[]{:S(2)}) collective-permute-start(f32[1,256]{1,0:T(1,128)S(1)} %add.3.mine_ref), channel_id=1, source_target_pairs={{0,3},{1,2},{2,1},{3,0},{4,7},{5,6},{6,5},{7,4},{8,11},{9,10},{10,... | collective-permute-start | bytes 3080 | tf_op jit(solution)/shard_map/ppermute | solution.py:325
  46.5 1.6 %copy-start = (f32[2048]{0:T(1024)S(1)}, f32[2048]{0:T(1024)}, u32[]{:S(2)}) copy-start(f32[2048]{0:T(1024)} %param.15) | copy-start | bytes 24580

commit v2 on v1

--- a/solution.py
+++ b/solution.py
@@ -10,7 +10,9 @@
 epsilon = 1e-06
 lanes = 128
 sublanes = 8
-piece_width = 512
+piece_width = 256
+pieces_beside = (2, 3, 3)
+send_order = ((1, 2, 0), (2, 0, 1), (1, 2, 0))
 vmem_bytes = 24 * 1024 * 1024
 
 
@@ -129,27 +131,27 @@
         base_ref[:, here] = x_ref[:, cols].astype(jnp.float32) + mixed
 
 
-def merge_kernel(size, rows, last, arrived_ref, decay_ref, *rest):
-    if size == 1:
-        total_ref, rest = rest[0], rest[1:]
-    elif last:
-        enter_ref, rest = rest[0], rest[1:]
-    else:
-        total_ref, enter_ref, rest = rest[0], rest[1], rest[2:]
+def merge_kernel(size, rows, order, first, last, decay_ref, total_ref, *rest):
     position = lax.axis_index("ctx")
-    arrived = arrived_ref[...].astype(jnp.float32)
+    odd = (position & size) != 0
+    high = (position & (2 * size)) != 0
     decay = decay_ref[...]
-    upper = (position & size) != 0
-    within = (position & (size - 1)).astype(jnp.float32) * float(rows)
-    share = jnp.where(upper, arrived, 0.0) * jnp.exp(decay * -within)
-    rest[0][...] = share if size == 1 else enter_ref[...] + share
+    near, far, across = (rest[order.index(at)][...].astype(jnp.float32) for at in range(3))
+    rest = rest[3:]
+    over = jnp.exp(decay * float(-rows * size))
+    other = jnp.where(odd, across * over + far, far * over + across)
+    enter = jnp.where(high, jnp.where(odd, other * over, other), 0.0) + jnp.where(odd, near, 0.0)
+    if not first:
+        within = (position & (size - 1)).astype(jnp.float32) * float(rows)
+        enter = rest[0][...] + enter * jnp.exp(decay * -within)
+        rest = rest[1:]
+    rest[0][...] = enter
     if not last:
-        over = jnp.exp(decay * float(-rows * size))
         total = total_ref[...]
-        total = jnp.where(upper, total + over * arrived, over * total + arrived)
-        rest[1][...] = total.astype(jnp.bfloat16)
-        if len(rest) > 2:
-            rest[2][...] = total
+        own = jnp.where(odd, near * over + total, total * over + near)
+        whole = jnp.where(high, other * (over * over) + own, own * (over * over) + other)
+        rest[1][...] = whole.astype(jnp.bfloat16)
+        rest[2][...] = whole
 
 
 def finish_kernel(enter_ref, tile_ref, v_ref, *rest):
@@ -271,19 +273,17 @@
         index = lambda z, y, x: (z * 2 + y) * 4 + x
         return [(index(*at), index(*partner_of(*at))) for at in places]
 
-    rounds = [
-        link(lambda z, y, x: (z, y, x ^ 1)),
-        link(lambda z, y, x: (z, y, x ^ 3)),
-        link(lambda z, y, x: (z, y ^ 1, x)),
-        link(lambda z, y, x: (z ^ 1, y, x)),
-        link(lambda z, y, x: (z ^ 2, y, x)),
-        link(lambda z, y, x: ((6, 7, 4, 5, 2, 3, 0, 1)[z], y, x)),
+    stages = [
+        [link(lambda z, y, x, k=k: (z, y, x ^ k)) for k in (1, 2, 3)],
+        [link(lambda z, y, x, k=k: (z ^ (k >> 1), y ^ (k & 1), x)) for k in (1, 2, 3)],
+        [link(lambda z, y, x, k=k: (z ^ k, y, x)) for k in (2, 5, 6)],
     ]
-    def merge(size, last, keep, arrived, total, enter):
-        operands = [arrived, decay] + ([] if last else [total]) + ([] if size == 1 else [enter])
-        outs = [f32] if last else [f32, bf16, f32] if keep else [f32, bf16]
+
+    def merge(size, order, last, total, arrived, enter):
+        operands = [decay, total, *arrived] + ([] if enter is None else [enter])
+        outs = [f32] if last else [f32, bf16, f32]
         return pl.pallas_call(
-            functools.partial(merge_kernel, size, rows, last),
+            functools.partial(merge_kernel, size, rows, order, enter is None, last),
             in_specs=[in_vmem] * len(operands),
             out_specs=[in_vmem] * len(outs),
             out_shape=[pltpu.VMEM((modes, width), dtype) for dtype in outs],
@@ -293,22 +293,19 @@
 
     enter = None
     bases, leads = [], []
-    for level, pairs in enumerate(rounds):
-        arrived = lax.ppermute(sent, "ctx", pairs)
-        if level < pieces:
-            tied, sent = lax.optimization_barrier((decay, sent))
-            base, lead = local_piece(level, tied)
-            arrived, base = lax.optimization_barrier((arrived, base))
-            bases.append(base)
-            leads.append(lead)
-        last = level + 1 == len(rounds)
-        keep = level + 2 < len(rounds)
-        merged = merge(1 << level, last, keep, arrived, total, enter)
+    for level, (links, beside) in enumerate(zip(stages, pieces_beside)):
+        order = send_order[level]
+        arrived = [lax.ppermute(sent, "ctx", links[at]) for at in order]
+        tied, sent = lax.optimization_barrier((decay, sent))
+        made = [local_piece(len(bases) + at, tied) for at in range(beside)]
+        arrived, made = lax.optimization_barrier((arrived, made))
+        bases += [base for base, _ in made]
+        leads += [lead for _, lead in made]
+        last = level + 1 == len(stages)
+        merged = merge(4**level, order, last, total, arrived, enter)
         enter = merged[0]
         if not last:
-            sent = merged[1]
-        if keep:
-            total = merged[2]
+            sent, total = merged[1:]
 
     fresh, power = pl.pallas_call(
         finish_kernel,

time: 49.5 us -> 46.3 us (0.935)
  waiting for transfers between devices: 5.48 us -> 3.36 us
  starting transfers between devices: 22.4 us -> 21.3 us
    ppermute x6 -> x9, waiting for transfers between devices: 4.08 us -> 2.14 us  [shards(): arrived = [lax.ppermute(sent, 'ctx', links[at]) for at in order]]
    ppermute x1, starting transfers between devices: 5.31 us -> 3.86 us  [shards(): power = power + lax.ppermute(power, 'tp', [(i, i ^ 1) for i in range(4)])]
    ppermute x6 -> x9, starting transfers between devices: 14.2 us -> 14.3 us  [shards(): arrived = [lax.ppermute(sent, 'ctx', links[at]) for at in order]]
    pallas_call x4 -> x8, Pallas kernels: 10.7 us -> 10.7 us  [local_piece(): pl.pallas_call(functools.partial(local_kernel, piece), in_specs=[in_vmem]...]
  transfers between devices with their start and end apart: 8 -> 11, of which waited for: 4 -> 5; matrix products, arithmetic and copies ran while one was open for 2% -> 2% of each run, Pallas kernels for 22% -> 23%
where the time goes in v2:
time: 46.3 us
  starting transfers between devices  21.3 us (46%)
  Pallas kernels  19.7 us (43%)
  waiting for transfers between devices  3.36 us (7%)
  local copies, waits for them, and re-layouts  0.97 us (2%)
  between operations  0.93 us (2%)
    ppermute x9, starting transfers between devices, shards(): arrived = [lax.ppermute(sent, 'ctx', links[at]) for at in order]  14.3 us
    pallas_call x8, Pallas kernels, local_piece(): pl.pallas_call(functools.partial(local_kernel, piece), in_specs=[in_vmem]...  10.7 us
    pallas_call x1, Pallas kernels, shards(): pl.pallas_call(state_kernel, in_specs=[anywhere] * len(far), out_specs=[i...  4.36 us
    ppermute x1, starting transfers between devices, shards(): power = power + lax.ppermute(power, 'tp', [(i, i ^ 1) for i in range(4)])  3.86 us
    ppermute x1, starting transfers between devices, shards(): other = lax.ppermute(power, 'tp', [(i, i ^ 3) for i in range(4)])  3.12 us
    pallas_call x1, Pallas kernels, shards(): pl.pallas_call(finish_kernel, in_specs=[in_vmem] * (3 + 2 * pieces), out_...  3.02 us
    ppermute x9, waiting for transfers between devices, shards(): arrived = [lax.ppermute(sent, 'ctx', links[at]) for at in order]  2.14 us
    pallas_call x1, Pallas kernels, shards(): pl.pallas_call(functools.partial(norm_kernel, channels), in_specs=[in_vme...  1.31 us
  transfers between devices with their start and end apart: 11, of which 5 were waited for; matrix products, arithmetic and copies ran while one was open for 2% of the time, Pallas kernels for 23%

profile of v2, /device:TPU:1, one launch (start us, length us, event | category | flops | bytes accessed | tf_op | source)
XLA Modules:
  0.0 46.3 jit_solution(8067521734643185852)
XLA Ops:
  0.6 4.4 %states.1 = (f32[16,2048]{1,0:T(8,128)S(1)}, bf16[16,2048]{1,0:T(8,128)(2,1)S(1)}, bf16[256,2048]{1,0:T(8,128)(2,1)S(1)}, bf16[256,2048]{1,0:T(8,128)(2,1)S(1)},...) custom-call(bf16[256,2048]{1,0:T(8,128)(2,1)} %q_hbm.1, ...), custom_call_target="tpu_custom_call" | custom-call | flops 16777216 | bytes 2097152 | tf_op jit(solution)/shard_map/states/pallas_call | solution.py:240
  5.0 3.7 %collective-permute-start = (bf16[16,2048]{1,0:T(8,128)(2,1)S(1)}, bf16[16,2048]{1,0:T(8,128)(2,1)S(1)}, u32[]{:S(2)}, u32[]{:S(2)}) collective-permute-start(bf16[16,2048]{1,0:T(8,128)(2,1)S(1)} %get-tuple-element.65), channel_id=1, source_target_pairs={{0,8},{4,12},{8,0},{12,4},{16,24},{20,28},{24,16},{28,20},{32,40},... | collective-permute-start | bytes 196616 | tf_op jit(solution)/shard_map/ppermute | solution.py:298
  8.7 0.9 %collective-permute-start.1 = (bf16[16,2048]{1,0:T(8,128)(2,1)S(1)}, bf16[16,2048]{1,0:T(8,128)(2,1)S(1)}, u32[]{:S(2)}, u32[]{:S(2)}) collective-permute-start(bf16[16,2048]{1,0:T(8,128)(2,1)S(1)} %get-tuple-element.65), channel_id=1, source_target_pairs={{0,12},{4,8},{8,4},{12,0},{16,28},{20,24},{24,20},{28,16},{32,44},... | collective-permute-start | bytes 196616 | tf_op jit(solution)/shard_map/ppermute | solution.py:298
  9.5 0.0 collective-permute-start.2
  9.5 1.3 %local.9 = (f32[256,256]{1,0:T(8,128)S(1)}, f32[16,8,256]{2,1,0:T(8,128)S(1)}) custom-call(f32[16,2048]{1,0:T(8,128)S(1)} %get-tuple-element.94.decay_ref, f32[16,2048]{1,0:T(8,128)S(1)} %get-tuple-element.67.res_ref, f32[1,2048]{1,0:T(1,128)S(1)} %get-tuple-element.68.skip_ref, bf16[256,2048]{1,0:T(8,128)(2,1)S(1)} %get-tuple-element.69.sig_ref, ...), custom_call_target="tpu_custom_call" | custom-call | flops 6291456 | bytes 786432 | tf_op jit(solution)/shard_map/local/pallas_call | solution.py:258
  10.9 1.3 %local.8 = (f32[256,256]{1,0:T(8,128)S(1)}, f32[16,8,256]{2,1,0:T(8,128)S(1)}) custom-call(f32[16,2048]{1,0:T(8,128)S(1)} %get-tuple-element.94.decay_ref, f32[16,2048]{1,0:T(8,128)S(1)} %get-tuple-element.67.res_ref, f32[1,2048]{1,0:T(1,128)S(1)} %get-tuple-element.68.skip_ref, bf16[256,2048]{1,0:T(8,128)(2,1)S(1)} %get-tuple-element.69.sig_ref, ...), custom_call_target="tpu_custom_call" | custom-call | flops 6291456 | bytes 786432 | tf_op jit(solution)/shard_map/local/pallas_call | solution.py:258
  12.2 0.0 collective-permute-done.rest_0_
  12.2 1.5 %collective-permute-done.1.rest_1_ = bf16[16,2048]{1,0:T(8,128)(2,1)S(1)} collective-permute-done((bf16[16,2048]{1,0:T(8,128)(2,1)S(1)}, bf16[16,2048]{1,0:T(8,128)(2,1)S(1)}, u32[]{:S(2)}, u32[]{:S(2)}) %collective-permute-start.1) | collective-permute-done | bytes 65568 | tf_op jit(solution)/shard_map/ppermute | solution.py:298
  13.7 0.0 collective-permute-done.2.rest_2_
  13.7 0.1 merge.3
  13.8 2.0 %collective-permute-start.3 = (bf16[16,2048]{1,0:T(8,128)(2,1)S(1)}, bf16[16,2048]{1,0:T(8,128)(2,1)S(1)}, u32[]{:S(2)}, u32[]{:S(2)}) collective-permute-start(bf16[16,2048]{1,0:T(8,128)(2,1)S(1)} %get-tuple-element.80), channel_id=1, source_target_pairs={{0,48},{4,52},{8,56},{12,60},{16,32},{20,36},{24,40},{28,44},{32,1... | collective-permute-start | bytes 196616 | tf_op jit(solution)/shard_map/ppermute | solution.py:298
  15.9 0.2 collective-permute-start.4
  16.0 0.5 %collective-permute-start.5 = (bf16[16,2048]{1,0:T(8,128)(2,1)S(1)}, bf16[16,2048]{1,0:T(8,128)(2,1)S(1)}, u32[]{:S(2)}, u32[]{:S(2)}) collective-permute-start(bf16[16,2048]{1,0:T(8,128)(2,1)S(1)} %get-tuple-element.80), channel_id=1, source_target_pairs={{0,32},{4,36},{8,40},{12,44},{16,48},{20,52},{24,56},{28,60},{32,0... | collective-permute-start | bytes 196616 | tf_op jit(solution)/shard_map/ppermute | solution.py:298
  16.6 1.3 %local.12 = (f32[256,256]{1,0:T(8,128)S(1)}, f32[16,8,256]{2,1,0:T(8,128)S(1)}) custom-call(f32[16,2048]{1,0:T(8,128)S(1)} %get-tuple-element.94.decay_ref, f32[16,2048]{1,0:T(8,128)S(1)} %get-tuple-element.67.res_ref, f32[1,2048]{1,0:T(1,128)S(1)} %get-tuple-element.68.skip_ref, bf16[256,2048]{1,0:T(8,128)(2,1)S(1)} %get-tuple-element.69.sig_ref, ...), custom_call_target="tpu_custom_call" | custom-call | flops 6291456 | bytes 786432 | tf_op jit(solution)/shard_map/local/pallas_call | solution.py:258
  17.9 1.3 %local.11 = (f32[256,256]{1,0:T(8,128)S(1)}, f32[16,8,256]{2,1,0:T(8,128)S(1)}) custom-call(f32[16,2048]{1,0:T(8,128)S(1)} %get-tuple-element.94.decay_ref, f32[16,2048]{1,0:T(8,128)S(1)} %get-tuple-element.67.res_ref, f32[1,2048]{1,0:T(1,128)S(1)} %get-tuple-element.68.skip_ref, bf16[256,2048]{1,0:T(8,128)(2,1)S(1)} %get-tuple-element.69.sig_ref, ...), custom_call_target="tpu_custom_call" | custom-call | flops 6291456 | bytes 786432 | tf_op jit(solution)/shard_map/local/pallas_call | solution.py:258
  19.3 1.3 %local.10 = (f32[256,256]{1,0:T(8,128)S(1)}, f32[16,8,256]{2,1,0:T(8,128)S(1)}) custom-call(f32[16,2048]{1,0:T(8,128)S(1)} %get-tuple-element.94.decay_ref, f32[16,2048]{1,0:T(8,128)S(1)} %get-tuple-element.67.res_ref, f32[1,2048]{1,0:T(1,128)S(1)} %get-tuple-element.68.skip_ref, bf16[256,2048]{1,0:T(8,128)(2,1)S(1)} %get-tuple-element.69.sig_ref, ...), custom_call_target="tpu_custom_call" | custom-call | flops 6291456 | bytes 786432 | tf_op jit(solution)/shard_map/local/pallas_call | solution.py:258
  20.6 0.0 collective-permute-done.3.rest_0_
  20.6 0.0 collective-permute-done.4.rest_1_
  20.6 0.0 collective-permute-done.5.rest_2_
  20.6 0.2 merge.4
  20.8 5.8 %collective-permute-start.6 = (bf16[16,2048]{1,0:T(8,128)(2,1)S(1)}, bf16[16,2048]{1,0:T(8,128)(2,1)S(1)}, u32[]{:S(2)}, u32[]{:S(2)}) collective-permute-start(bf16[16,2048]{1,0:T(8,128)(2,1)S(1)} %get-tuple-element.93), channel_id=1, source_target_pairs={{0,160},{4,164},{8,168},{12,172},{16,176},{20,180},{24,184},{28,18... | collective-permute-start | bytes 196616 | tf_op jit(solution)/shard_map/ppermute | solution.py:298
  26.6 0.3 collective-permute-start.7
  26.9 0.9 %collective-permute-start.8 = (bf16[16,2048]{1,0:T(8,128)(2,1)S(1)}, bf16[16,2048]{1,0:T(8,128)(2,1)S(1)}, u32[]{:S(2)}, u32[]{:S(2)}) collective-permute-start(bf16[16,2048]{1,0:T(8,128)(2,1)S(1)} %get-tuple-element.93), channel_id=1, source_target_pairs={{0,64},{4,68},{8,72},{12,76},{16,80},{20,84},{24,88},{28,92},{32,9... | collective-permute-start | bytes 196616 | tf_op jit(solution)/shard_map/ppermute | solution.py:298
  27.8 1.3 %local.15 = (f32[256,256]{1,0:T(8,128)S(1)}, f32[16,8,256]{2,1,0:T(8,128)S(1)}) custom-call(f32[16,2048]{1,0:T(8,128)S(1)} %get-tuple-element.94.decay_ref, f32[16,2048]{1,0:T(8,128)S(1)} %get-tuple-element.67.res_ref, f32[1,2048]{1,0:T(1,128)S(1)} %get-tuple-element.68.skip_ref, bf16[256,2048]{1,0:T(8,128)(2,1)S(1)} %get-tuple-element.69.sig_ref, ...), custom_call_target="tpu_custom_call" | custom-call | flops 6291456 | bytes 786432 | tf_op jit(solution)/shard_map/local/pallas_call | solution.py:258
  29.1 1.3 %local.14 = (f32[256,256]{1,0:T(8,128)S(1)}, f32[16,8,256]{2,1,0:T(8,128)S(1)}) custom-call(f32[16,2048]{1,0:T(8,128)S(1)} %get-tuple-element.94.decay_ref, f32[16,2048]{1,0:T(8,128)S(1)} %get-tuple-element.67.res_ref, f32[1,2048]{1,0:T(1,128)S(1)} %get-tuple-element.68.skip_ref, bf16[256,2048]{1,0:T(8,128)(2,1)S(1)} %get-tuple-element.69.sig_ref, ...), custom_call_target="tpu_custom_call" | custom-call | flops 6291456 | bytes 786432 | tf_op jit(solution)/shard_map/local/pallas_call | solution.py:258
  30.5 1.3 %local.13 = (f32[256,256]{1,0:T(8,128)S(1)}, f32[16,8,256]{2,1,0:T(8,128)S(1)}) custom-call(f32[16,2048]{1,0:T(8,128)S(1)} %get-tuple-element.94.decay_ref, f32[16,2048]{1,0:T(8,128)S(1)} %get-tuple-element.67.res_ref, f32[1,2048]{1,0:T(1,128)S(1)} %get-tuple-element.68.skip_ref, bf16[256,2048]{1,0:T(8,128)(2,1)S(1)} %get-tuple-element.69.sig_ref, ...), custom_call_target="tpu_custom_call" | custom-call | flops 6291456 | bytes 786432 | tf_op jit(solution)/shard_map/local/pallas_call | solution.py:258
  31.8 0.0 collective-permute-done.6.rest_0_
  31.8 0.4 collective-permute-done.7.rest_1_
  32.2 0.3 collective-permute-done.8.rest_2_
  32.5 0.1 merge.5.enter_ref
  32.6 3.0 %finish.1 = (bf16[256,2048]{1,0:T(8,128)(2,1)S(1)}, f32[1,256]{1,0:T(1,128)S(1)}) custom-call(f32[16,2048]{1,0:T(8,128)S(1)} %merge.5.enter_ref, f32[16,2048]{1,0:T(8,128)S(1)} %get-tuple-element.105.tile_ref, bf16[256,2048]{1,0:T(8,128)(2,1)S(1)} %get-tuple-element.70.v_ref, f32[256,256]{1,0:T(8,128)S(1)} %get-tuple-element.106.rest_0_, ...), custom_call_target="tpu_custom_call" | custom-call | flops 16777216 | bytes 4194304 | tf_op jit(solution)/shard_map/finish/pallas_call | solution.py:310
  35.6 3.9 %collective-permute-start.9 = (f32[1,256]{1,0:T(1,128)S(1)}, f32[1,256]{1,0:T(1,128)S(1)}, u32[]{:S(2)}, u32[]{:S(2)}) collective-permute-start(f32[1,256]{1,0:T(1,128)S(1)} %get-tuple-element.123), channel_id=1, source_target_pairs={{0,1},{1,0},{2,3},{3,2},{4,5},{5,4},{6,7},{7,6},{8,9},{9,8},{10,11... | collective-permute-start | bytes 3080 | tf_op jit(solution)/shard_map/ppermute | solution.py:321
  39.5 0.8 %collective-permute-done.9 = f32[1,256]{1,0:T(1,128)S(1)} collective-permute-done((f32[1,256]{1,0:T(1,128)S(1)}, f32[1,256]{1,0:T(1,128)S(1)}, u32[]{:S(2)}, u32[]{:S(2)}) %collective-permute-start.9) | collective-permute-done | bytes 1056 | tf_op jit(solution)/shard_map/ppermute | solution.py:321
  40.3 3.1 %collective-permute-start.10 = (f32[1,256]{1,0:T(1,128)S(1)}, f32[1,256]{1,0:T(1,128)S(1)}, u32[]{:S(2)}, u32[]{:S(2)}) collective-permute-start(f32[1,256]{1,0:T(1,128)S(1)} %add.3.mine_ref), channel_id=1, source_target_pairs={{0,3},{1,2},{2,1},{3,0},{4,7},{5,6},{6,5},{7,4},{8,11},{9,10},{10,... | collective-permute-start | bytes 3080 | tf_op jit(solution)/shard_map/ppermute | solution.py:322
  43.4 0.0 copy-start
  43.4 1.0 %copy.10 = bf16[256,2048]{1,0:T(8,128)(2,1)} copy(bf16[256,2048]{1,0:T(8,128)(2,1)S(1)} %get-tuple-element.124.new_ref) | data formatting | bytes 2097152
  44.4 0.4 collective-permute-done.10.other_ref
  44.8 0.0 copy-done
  44.8 1.3 %normalise.1 = bf16[256,2048]{1,0:T(8,128)(2,1)} custom-call(f32[1,256]{1,0:T(1,128)S(1)} %add.3.mine_ref, f32[1,256]{1,0:T(1,128)S(1)} %collective-permute-done.10.other_ref, f32[1,2048]{1,0:T(1,128)S(1)} %bitcast.2, bf16[256,2048]{1,0:T(8,128)(2,1)S(1)} %get-tuple-element.124.new_ref), custom_call_target="tpu_custom_call" | custom-call | tf_op jit(solution)/shard_map/normalise/pallas_call | solution.py:325
  (1 shorter events, 0.0 us)
Async XLA Ops:
  5.0 7.2 %collective-permute-start = (bf16[16,2048]{1,0:T(8,128)(2,1)S(1)}, bf16[16,2048]{1,0:T(8,128)(2,1)S(1)}, u32[]{:S(2)}, u32[]{:S(2)}) collective-permute-start(bf16[16,2048]{1,0:T(8,128)(2,1)S(1)} %get-tuple-element.65), channel_id=1, source_target_pairs={{0,8},{4,12},{8,0},{12,4},{16,24},{20,28},{24,16},{28,20},{32,40},... | collective-permute-start | bytes 196616 | tf_op jit(solution)/shard_map/ppermute | solution.py:298
  8.7 5.0 %collective-permute-start.1 = (bf16[16,2048]{1,0:T(8,128)(2,1)S(1)}, bf16[16,2048]{1,0:T(8,128)(2,1)S(1)}, u32[]{:S(2)}, u32[]{:S(2)}) collective-permute-start(bf16[16,2048]{1,0:T(8,128)(2,1)S(1)} %get-tuple-element.65), channel_id=1, source_target_pairs={{0,12},{4,8},{8,4},{12,0},{16,28},{20,24},{24,20},{28,16},{32,44},... | collective-permute-start | bytes 196616 | tf_op jit(solution)/shard_map/ppermute | solution.py:298
  9.5 4.2 %collective-permute-start.2 = (bf16[16,2048]{1,0:T(8,128)(2,1)S(1)}, bf16[16,2048]{1,0:T(8,128)(2,1)S(1)}, u32[]{:S(2)}, u32[]{:S(2)}) collective-permute-start(bf16[16,2048]{1,0:T(8,128)(2,1)S(1)} %get-tuple-element.65), channel_id=1, source_target_pairs={{0,4},{4,0},{8,12},{12,8},{16,20},{20,16},{24,28},{28,24},{32,36},... | collective-permute-start | bytes 196616 | tf_op jit(solution)/shard_map/ppermute | solution.py:298
  13.8 6.8 %collective-permute-start.3 = (bf16[16,2048]{1,0:T(8,128)(2,1)S(1)}, bf16[16,2048]{1,0:T(8,128)(2,1)S(1)}, u32[]{:S(2)}, u32[]{:S(2)}) collective-permute-start(bf16[16,2048]{1,0:T(8,128)(2,1)S(1)} %get-tuple-element.80), channel_id=1, source_target_pairs={{0,48},{4,52},{8,56},{12,60},{16,32},{20,36},{24,40},{28,44},{32,1... | collective-permute-start | bytes 196616 | tf_op jit(solution)/shard_map/ppermute | solution.py:298
  15.9 4.7 %collective-permute-start.4 = (bf16[16,2048]{1,0:T(8,128)(2,1)S(1)}, bf16[16,2048]{1,0:T(8,128)(2,1)S(1)}, u32[]{:S(2)}, u32[]{:S(2)}) collective-permute-start(bf16[16,2048]{1,0:T(8,128)(2,1)S(1)} %get-tuple-element.80), channel_id=1, source_target_pairs={{0,16},{4,20},{8,24},{12,28},{16,0},{20,4},{24,8},{28,12},{32,48},... | collective-permute-start | bytes 196616 | tf_op jit(solution)/shard_map/ppermute | solution.py:298
  16.0 4.6 %collective-permute-start.5 = (bf16[16,2048]{1,0:T(8,128)(2,1)S(1)}, bf16[16,2048]{1,0:T(8,128)(2,1)S(1)}, u32[]{:S(2)}, u32[]{:S(2)}) collective-permute-start(bf16[16,2048]{1,0:T(8,128)(2,1)S(1)} %get-tuple-element.80), channel_id=1, source_target_pairs={{0,32},{4,36},{8,40},{12,44},{16,48},{20,52},{24,56},{28,60},{32,0... | collective-permute-start | bytes 196616 | tf_op jit(solution)/shard_map/ppermute | solution.py:298
  20.8 11.0 %collective-permute-start.6 = (bf16[16,2048]{1,0:T(8,128)(2,1)S(1)}, bf16[16,2048]{1,0:T(8,128)(2,1)S(1)}, u32[]{:S(2)}, u32[]{:S(2)}) collective-permute-start(bf16[16,2048]{1,0:T(8,128)(2,1)S(1)} %get-tuple-element.93), channel_id=1, source_target_pairs={{0,160},{4,164},{8,168},{12,172},{16,176},{20,180},{24,184},{28,18... | collective-permute-start | bytes 196616 | tf_op jit(solution)/shard_map/ppermute | solution.py:298
  26.6 5.6 %collective-permute-start.7 = (bf16[16,2048]{1,0:T(8,128)(2,1)S(1)}, bf16[16,2048]{1,0:T(8,128)(2,1)S(1)}, u32[]{:S(2)}, u32[]{:S(2)}) collective-permute-start(bf16[16,2048]{1,0:T(8,128)(2,1)S(1)} %get-tuple-element.93), channel_id=1, source_target_pairs={{0,192},{4,196},{8,200},{12,204},{16,208},{20,212},{24,216},{28,22... | collective-permute-start | bytes 196616 | tf_op jit(solution)/shard_map/ppermute | solution.py:298
  26.9 5.6 %collective-permute-start.8 = (bf16[16,2048]{1,0:T(8,128)(2,1)S(1)}, bf16[16,2048]{1,0:T(8,128)(2,1)S(1)}, u32[]{:S(2)}, u32[]{:S(2)}) collective-permute-start(bf16[16,2048]{1,0:T(8,128)(2,1)S(1)} %get-tuple-element.93), channel_id=1, source_target_pairs={{0,64},{4,68},{8,72},{12,76},{16,80},{20,84},{24,88},{28,92},{32,9... | collective-permute-start | bytes 196616 | tf_op jit(solution)/shard_map/ppermute | solution.py:298
  35.6 4.7 %collective-permute-start.9 = (f32[1,256]{1,0:T(1,128)S(1)}, f32[1,256]{1,0:T(1,128)S(1)}, u32[]{:S(2)}, u32[]{:S(2)}) collective-permute-start(f32[1,256]{1,0:T(1,128)S(1)} %get-tuple-element.123), channel_id=1, source_target_pairs={{0,1},{1,0},{2,3},{3,2},{4,5},{5,4},{6,7},{7,6},{8,9},{9,8},{10,11... | collective-permute-start | bytes 3080 | tf_op jit(solution)/shard_map/ppermute | solution.py:321
  40.3 4.5 %collective-permute-start.10 = (f32[1,256]{1,0:T(1,128)S(1)}, f32[1,256]{1,0:T(1,128)S(1)}, u32[]{:S(2)}, u32[]{:S(2)}) collective-permute-start(f32[1,256]{1,0:T(1,128)S(1)} %add.3.mine_ref), channel_id=1, source_target_pairs={{0,3},{1,2},{2,1},{3,0},{4,7},{5,6},{6,5},{7,4},{8,11},{9,10},{10,... | collective-permute-start | bytes 3080 | tf_op jit(solution)/shard_map/ppermute | solution.py:322
  43.4 1.4 %copy-start = (f32[2048]{0:T(1024)S(1)}, f32[2048]{0:T(1024)}, u32[]{:S(2)}) copy-start(f32[2048]{0:T(1024)} %param.15) | copy-start | bytes 24580

commit v3 on v2

--- a/solution.py
+++ b/solution.py
@@ -38,7 +38,7 @@
 ):
     modes = decay_ref.shape[0]
     rows, width = q_ref.shape
-    edges = [0, 256, 512] + list(range(1024, width + 1, 512))
+    edges = [0, 256, 1024, width]
     pair = []
     first = pltpu.make_async_copy(decay_hbm, decay_ref, side_sem.at[0])
     first.start()
@@ -60,7 +60,7 @@
         pair[2 * p].wait()
         pair[2 * p + 1].wait()
 
-        @pl.loop(low // lanes, high // lanes)
+        @pl.loop(low // lanes, high // lanes, unroll=2)
         def _(group):
             cols = at_group(group)
             steps = [spread(tile_ref, n, cols) for n in range(modes)]
@@ -173,7 +173,8 @@
                 halves = []
                 for half in range(2):
                     halves.append(tree_sum(states))
-                    states = [s * a for s, a in zip(states, steps)]
+                    if pair * 2 + half + 1 < rows // sublanes:
+                        states = [s * a for s, a in zip(states, steps)]
                 at = pl.ds(pair * 2 * sublanes, 2 * sublanes)
                 carried = jnp.concatenate(halves, axis=0)
                 fresh = base_ref[at, here] + v_ref[at, cols].astype(jnp.float32) * carried
@@ -182,14 +183,13 @@
                 fresh = fresh.astype(jnp.float32)
                 acc_ref[at, :] += fresh * fresh
 
-    ones = jnp.ones((sublanes, lanes), jnp.float32)
-    sums = lax.dot_general(
-        ones,
-        acc_ref[...],
-        (((1,), (1,)), ((), ())),
-        precision=lax.Precision.HIGHEST,
-        preferred_element_type=jnp.float32,
-    )
+    ones = jnp.ones((2 * sublanes, lanes), jnp.bfloat16)
+    rest = acc_ref[...]
+    sums = jnp.zeros((2 * sublanes, rows), jnp.float32)
+    for _ in range(3):
+        head = rest.astype(jnp.bfloat16)
+        rest = rest - head.astype(jnp.float32)
+        sums += lax.dot_general(ones, head, (((1,), (1,)), ((), ())), preferred_element_type=jnp.float32)
     power_ref[...] = sums[0:1]
 
 
@@ -198,21 +198,23 @@
     power = (mine_ref[...] + other_ref[...]) * (1.0 / channels)
     inverse = lax.rsqrt(power + epsilon)
     inv_ref[...] = jnp.transpose(jnp.broadcast_to(inverse, (lanes, rows)))
-    copies = []
     part = width // sem.shape[0]
-    for p in range(sem.shape[0]):
-
-        @pl.loop(p * part // lanes, (p + 1) * part // lanes)
-        def _(group):
-            cols = at_group(group)
+
+    def written(p):
+        cols = pl.ds(pl.multiple_of(p * part, part), part)
+        return pltpu.make_async_copy(out_ref.at[:, cols], out_hbm.at[:, cols], sem.at[p])
+
+    @pl.loop(0, sem.shape[0])
+    def _(p):
+        for group in range(part // lanes):
+            cols = at_group(p * (part // lanes) + group)
             scaled = new_ref[:, cols].astype(jnp.float32) * inv_ref[...] * gain_ref[:, cols]
             out_ref[:, cols] = scaled.astype(jnp.bfloat16)
-
-        cols = pl.ds(p * part, part)
-        copies.append(pltpu.make_async_copy(out_ref.at[:, cols], out_hbm.at[:, cols], sem.at[p]))
-        copies[-1].start()
-    for copy in copies:
-        copy.wait()
+        written(p).start()
+
+    @pl.loop(0, sem.shape[0])
+    def _(p):
+        written(p).wait()
 
 
 def shards(queries, key_proj, values, residues, decay_rates, skip_weight, stream, norm_gain):

time: 46.3 us -> 45.9 us (level)
  Pallas kernels: 19.7 us -> 19.2 us
where the time goes in v3:
time: 45.9 us; the launch traced here: 45.8 us
  starting transfers between devices  21.3 us (46%)
  Pallas kernels  19.2 us (42%)
  waiting for transfers between devices  3.36 us (7%)
  local copies, waits for them, and re-layouts  0.97 us (2%)
  between operations  0.93 us (2%)
    ppermute x9, starting transfers between devices, shards(): arrived = [lax.ppermute(sent, 'ctx', links[at]) for at in order]  14.3 us
    pallas_call x8, Pallas kernels, local_piece(): pl.pallas_call(functools.partial(local_kernel, piece), in_specs=[in_vmem]...  10.7 us
    pallas_call x1, Pallas kernels, shards(): pl.pallas_call(state_kernel, in_specs=[anywhere] * len(far), out_specs=[i...  3.98 us
    ppermute x1, starting transfers between devices, shards(): power = power + lax.ppermute(power, 'tp', [(i, i ^ 1) for i in range(4)])  3.89 us
    ppermute x1, starting transfers between devices, shards(): other = lax.ppermute(power, 'tp', [(i, i ^ 3) for i in range(4)])  3.12 us
    pallas_call x1, Pallas kernels, shards(): pl.pallas_call(finish_kernel, in_specs=[in_vmem] * (3 + 2 * pieces), out_...  2.95 us
    ppermute x9, waiting for transfers between devices, shards(): arrived = [lax.ppermute(sent, 'ctx', links[at]) for at in order]  2.14 us
    pallas_call x1, Pallas kernels, shards(): pl.pallas_call(functools.partial(norm_kernel, channels), in_specs=[in_vme...  1.24 us
  transfers between devices with their start and end apart: 11, of which 5 were waited for; matrix products, arithmetic and copies ran while one was open for 2% of the time, Pallas kernels for 23%

profile of v3, /device:TPU:1, one launch (start us, length us, event | category | flops | bytes accessed | tf_op | source)
XLA Modules:
  0.0 45.8 jit_solution(6136884761502627802)
XLA Ops:
  0.6 4.0 %states.1 = (f32[16,2048]{1,0:T(8,128)S(1)}, bf16[16,2048]{1,0:T(8,128)(2,1)S(1)}, bf16[256,2048]{1,0:T(8,128)(2,1)S(1)}, bf16[256,2048]{1,0:T(8,128)(2,1)S(1)},...) custom-call(bf16[256,2048]{1,0:T(8,128)(2,1)} %q_hbm.1, ...), custom_call_target="tpu_custom_call" | custom-call | flops 16777216 | bytes 2097152 | tf_op jit(solution)/shard_map/states/pallas_call | solution.py:242
  4.6 3.7 %collective-permute-start = (bf16[16,2048]{1,0:T(8,128)(2,1)S(1)}, bf16[16,2048]{1,0:T(8,128)(2,1)S(1)}, u32[]{:S(2)}, u32[]{:S(2)}) collective-permute-start(bf16[16,2048]{1,0:T(8,128)(2,1)S(1)} %get-tuple-element.65), channel_id=1, source_target_pairs={{0,8},{4,12},{8,0},{12,4},{16,24},{20,28},{24,16},{28,20},{32,40},... | collective-permute-start | bytes 196616 | tf_op jit(solution)/shard_map/ppermute | solution.py:300
  8.3 0.9 %collective-permute-start.1 = (bf16[16,2048]{1,0:T(8,128)(2,1)S(1)}, bf16[16,2048]{1,0:T(8,128)(2,1)S(1)}, u32[]{:S(2)}, u32[]{:S(2)}) collective-permute-start(bf16[16,2048]{1,0:T(8,128)(2,1)S(1)} %get-tuple-element.65), channel_id=1, source_target_pairs={{0,12},{4,8},{8,4},{12,0},{16,28},{20,24},{24,20},{28,16},{32,44},... | collective-permute-start | bytes 196616 | tf_op jit(solution)/shard_map/ppermute | solution.py:300
  9.1 0.0 collective-permute-start.2
  9.1 1.3 %local.9 = (f32[256,256]{1,0:T(8,128)S(1)}, f32[16,8,256]{2,1,0:T(8,128)S(1)}) custom-call(f32[16,2048]{1,0:T(8,128)S(1)} %get-tuple-element.94.decay_ref, f32[16,2048]{1,0:T(8,128)S(1)} %get-tuple-element.67.res_ref, f32[1,2048]{1,0:T(1,128)S(1)} %get-tuple-element.68.skip_ref, bf16[256,2048]{1,0:T(8,128)(2,1)S(1)} %get-tuple-element.69.sig_ref, ...), custom_call_target="tpu_custom_call" | custom-call | flops 6291456 | bytes 786432 | tf_op jit(solution)/shard_map/local/pallas_call | solution.py:260
  10.5 1.3 %local.8 = (f32[256,256]{1,0:T(8,128)S(1)}, f32[16,8,256]{2,1,0:T(8,128)S(1)}) custom-call(f32[16,2048]{1,0:T(8,128)S(1)} %get-tuple-element.94.decay_ref, f32[16,2048]{1,0:T(8,128)S(1)} %get-tuple-element.67.res_ref, f32[1,2048]{1,0:T(1,128)S(1)} %get-tuple-element.68.skip_ref, bf16[256,2048]{1,0:T(8,128)(2,1)S(1)} %get-tuple-element.69.sig_ref, ...), custom_call_target="tpu_custom_call" | custom-call | flops 6291456 | bytes 786432 | tf_op jit(solution)/shard_map/local/pallas_call | solution.py:260
  11.8 0.0 collective-permute-done.rest_0_
  11.8 1.5 %collective-permute-done.1.rest_1_ = bf16[16,2048]{1,0:T(8,128)(2,1)S(1)} collective-permute-done((bf16[16,2048]{1,0:T(8,128)(2,1)S(1)}, bf16[16,2048]{1,0:T(8,128)(2,1)S(1)}, u32[]{:S(2)}, u32[]{:S(2)}) %collective-permute-start.1) | collective-permute-done | bytes 65568 | tf_op jit(solution)/shard_map/ppermute | solution.py:300
  13.3 0.0 collective-permute-done.2.rest_2_
  13.3 0.1 merge.3
  13.5 2.0 %collective-permute-start.3 = (bf16[16,2048]{1,0:T(8,128)(2,1)S(1)}, bf16[16,2048]{1,0:T(8,128)(2,1)S(1)}, u32[]{:S(2)}, u32[]{:S(2)}) collective-permute-start(bf16[16,2048]{1,0:T(8,128)(2,1)S(1)} %get-tuple-element.80), channel_id=1, source_target_pairs={{0,48},{4,52},{8,56},{12,60},{16,32},{20,36},{24,40},{28,44},{32,1... | collective-permute-start | bytes 196616 | tf_op jit(solution)/shard_map/ppermute | solution.py:300
  15.5 0.2 collective-permute-start.4
  15.7 0.5 %collective-permute-start.5 = (bf16[16,2048]{1,0:T(8,128)(2,1)S(1)}, bf16[16,2048]{1,0:T(8,128)(2,1)S(1)}, u32[]{:S(2)}, u32[]{:S(2)}) collective-permute-start(bf16[16,2048]{1,0:T(8,128)(2,1)S(1)} %get-tuple-element.80), channel_id=1, source_target_pairs={{0,32},{4,36},{8,40},{12,44},{16,48},{20,52},{24,56},{28,60},{32,0... | collective-permute-start | bytes 196616 | tf_op jit(solution)/shard_map/ppermute | solution.py:300
  16.2 1.3 %local.12 = (f32[256,256]{1,0:T(8,128)S(1)}, f32[16,8,256]{2,1,0:T(8,128)S(1)}) custom-call(f32[16,2048]{1,0:T(8,128)S(1)} %get-tuple-element.94.decay_ref, f32[16,2048]{1,0:T(8,128)S(1)} %get-tuple-element.67.res_ref, f32[1,2048]{1,0:T(1,128)S(1)} %get-tuple-element.68.skip_ref, bf16[256,2048]{1,0:T(8,128)(2,1)S(1)} %get-tuple-element.69.sig_ref, ...), custom_call_target="tpu_custom_call" | custom-call | flops 6291456 | bytes 786432 | tf_op jit(solution)/shard_map/local/pallas_call | solution.py:260
  17.5 1.3 %local.11 = (f32[256,256]{1,0:T(8,128)S(1)}, f32[16,8,256]{2,1,0:T(8,128)S(1)}) custom-call(f32[16,2048]{1,0:T(8,128)S(1)} %get-tuple-element.94.decay_ref, f32[16,2048]{1,0:T(8,128)S(1)} %get-tuple-element.67.res_ref, f32[1,2048]{1,0:T(1,128)S(1)} %get-tuple-element.68.skip_ref, bf16[256,2048]{1,0:T(8,128)(2,1)S(1)} %get-tuple-element.69.sig_ref, ...), custom_call_target="tpu_custom_call" | custom-call | flops 6291456 | bytes 786432 | tf_op jit(solution)/shard_map/local/pallas_call | solution.py:260
  18.9 1.3 %local.10 = (f32[256,256]{1,0:T(8,128)S(1)}, f32[16,8,256]{2,1,0:T(8,128)S(1)}) custom-call(f32[16,2048]{1,0:T(8,128)S(1)} %get-tuple-element.94.decay_ref, f32[16,2048]{1,0:T(8,128)S(1)} %get-tuple-element.67.res_ref, f32[1,2048]{1,0:T(1,128)S(1)} %get-tuple-element.68.skip_ref, bf16[256,2048]{1,0:T(8,128)(2,1)S(1)} %get-tuple-element.69.sig_ref, ...), custom_call_target="tpu_custom_call" | custom-call | flops 6291456 | bytes 786432 | tf_op jit(solution)/shard_map/local/pallas_call | solution.py:260
  20.2 0.0 collective-permute-done.3.rest_0_
  20.2 0.0 collective-permute-done.4.rest_1_
  20.2 0.0 collective-permute-done.5.rest_2_
  20.2 0.2 merge.4
  20.4 5.8 %collective-permute-start.6 = (bf16[16,2048]{1,0:T(8,128)(2,1)S(1)}, bf16[16,2048]{1,0:T(8,128)(2,1)S(1)}, u32[]{:S(2)}, u32[]{:S(2)}) collective-permute-start(bf16[16,2048]{1,0:T(8,128)(2,1)S(1)} %get-tuple-element.93), channel_id=1, source_target_pairs={{0,160},{4,164},{8,168},{12,172},{16,176},{20,180},{24,184},{28,18... | collective-permute-start | bytes 196616 | tf_op jit(solution)/shard_map/ppermute | solution.py:300
  26.2 0.3 collective-permute-start.7
  26.5 0.9 %collective-permute-start.8 = (bf16[16,2048]{1,0:T(8,128)(2,1)S(1)}, bf16[16,2048]{1,0:T(8,128)(2,1)S(1)}, u32[]{:S(2)}, u32[]{:S(2)}) collective-permute-start(bf16[16,2048]{1,0:T(8,128)(2,1)S(1)} %get-tuple-element.93), channel_id=1, source_target_pairs={{0,64},{4,68},{8,72},{12,76},{16,80},{20,84},{24,88},{28,92},{32,9... | collective-permute-start | bytes 196616 | tf_op jit(solution)/shard_map/ppermute | solution.py:300
  27.4 1.3 %local.15 = (f32[256,256]{1,0:T(8,128)S(1)}, f32[16,8,256]{2,1,0:T(8,128)S(1)}) custom-call(f32[16,2048]{1,0:T(8,128)S(1)} %get-tuple-element.94.decay_ref, f32[16,2048]{1,0:T(8,128)S(1)} %get-tuple-element.67.res_ref, f32[1,2048]{1,0:T(1,128)S(1)} %get-tuple-element.68.skip_ref, bf16[256,2048]{1,0:T(8,128)(2,1)S(1)} %get-tuple-element.69.sig_ref, ...), custom_call_target="tpu_custom_call" | custom-call | flops 6291456 | bytes 786432 | tf_op jit(solution)/shard_map/local/pallas_call | solution.py:260
  28.8 1.3 %local.14 = (f32[256,256]{1,0:T(8,128)S(1)}, f32[16,8,256]{2,1,0:T(8,128)S(1)}) custom-call(f32[16,2048]{1,0:T(8,128)S(1)} %get-tuple-element.94.decay_ref, f32[16,2048]{1,0:T(8,128)S(1)} %get-tuple-element.67.res_ref, f32[1,2048]{1,0:T(1,128)S(1)} %get-tuple-element.68.skip_ref, bf16[256,2048]{1,0:T(8,128)(2,1)S(1)} %get-tuple-element.69.sig_ref, ...), custom_call_target="tpu_custom_call" | custom-call | flops 6291456 | bytes 786432 | tf_op jit(solution)/shard_map/local/pallas_call | solution.py:260
  30.1 1.3 %local.13 = (f32[256,256]{1,0:T(8,128)S(1)}, f32[16,8,256]{2,1,0:T(8,128)S(1)}) custom-call(f32[16,2048]{1,0:T(8,128)S(1)} %get-tuple-element.94.decay_ref, f32[16,2048]{1,0:T(8,128)S(1)} %get-tuple-element.67.res_ref, f32[1,2048]{1,0:T(1,128)S(1)} %get-tuple-element.68.skip_ref, bf16[256,2048]{1,0:T(8,128)(2,1)S(1)} %get-tuple-element.69.sig_ref, ...), custom_call_target="tpu_custom_call" | custom-call | flops 6291456 | bytes 786432 | tf_op jit(solution)/shard_map/local/pallas_call | solution.py:260
  31.4 0.0 collective-permute-done.6.rest_0_
  31.5 0.4 collective-permute-done.7.rest_1_
  31.8 0.3 collective-permute-done.8.rest_2_
  32.1 0.1 merge.5.enter_ref
  32.2 3.0 %finish.1 = (bf16[256,2048]{1,0:T(8,128)(2,1)S(1)}, f32[1,256]{1,0:T(1,128)S(1)}) custom-call(f32[16,2048]{1,0:T(8,128)S(1)} %merge.5.enter_ref, f32[16,2048]{1,0:T(8,128)S(1)} %get-tuple-element.105.tile_ref, bf16[256,2048]{1,0:T(8,128)(2,1)S(1)} %get-tuple-element.70.v_ref, f32[256,256]{1,0:T(8,128)S(1)} %get-tuple-element.106.rest_0_, ...), custom_call_target="tpu_custom_call" | custom-call | flops 16777216 | bytes 4194304 | tf_op jit(solution)/shard_map/finish/pallas_call | solution.py:312
  35.2 3.9 %collective-permute-start.9 = (f32[1,256]{1,0:T(1,128)S(1)}, f32[1,256]{1,0:T(1,128)S(1)}, u32[]{:S(2)}, u32[]{:S(2)}) collective-permute-start(f32[1,256]{1,0:T(1,128)S(1)} %get-tuple-element.123), channel_id=1, source_target_pairs={{0,1},{1,0},{2,3},{3,2},{4,5},{5,4},{6,7},{7,6},{8,9},{9,8},{10,11... | collective-permute-start | bytes 3080 | tf_op jit(solution)/shard_map/ppermute | solution.py:323
  39.1 0.8 %collective-permute-done.9 = f32[1,256]{1,0:T(1,128)S(1)} collective-permute-done((f32[1,256]{1,0:T(1,128)S(1)}, f32[1,256]{1,0:T(1,128)S(1)}, u32[]{:S(2)}, u32[]{:S(2)}) %collective-permute-start.9) | collective-permute-done | bytes 1056 | tf_op jit(solution)/shard_map/ppermute | solution.py:323
  39.9 3.1 %collective-permute-start.10 = (f32[1,256]{1,0:T(1,128)S(1)}, f32[1,256]{1,0:T(1,128)S(1)}, u32[]{:S(2)}, u32[]{:S(2)}) collective-permute-start(f32[1,256]{1,0:T(1,128)S(1)} %add.3.mine_ref), channel_id=1, source_target_pairs={{0,3},{1,2},{2,1},{3,0},{4,7},{5,6},{6,5},{7,4},{8,11},{9,10},{10,... | collective-permute-start | bytes 3080 | tf_op jit(solution)/shard_map/ppermute | solution.py:324
  43.0 0.0 copy-start
  43.0 1.0 %copy.10 = bf16[256,2048]{1,0:T(8,128)(2,1)} copy(bf16[256,2048]{1,0:T(8,128)(2,1)S(1)} %get-tuple-element.124.new_ref) | data formatting | bytes 2097152
  44.0 0.4 collective-permute-done.10.other_ref
  44.4 0.0 copy-done
  44.4 1.2 %normalise.1 = bf16[256,2048]{1,0:T(8,128)(2,1)} custom-call(f32[1,256]{1,0:T(1,128)S(1)} %add.3.mine_ref, f32[1,256]{1,0:T(1,128)S(1)} %collective-permute-done.10.other_ref, f32[1,2048]{1,0:T(1,128)S(1)} %bitcast.2, bf16[256,2048]{1,0:T(8,128)(2,1)S(1)} %get-tuple-element.124.new_ref), custom_call_target="tpu_custom_call" | custom-call | tf_op jit(solution)/shard_map/normalise/pallas_call | solution.py:327
  (1 shorter events, 0.0 us)
Async XLA Ops:
  4.6 7.2 %collective-permute-start = (bf16[16,2048]{1,0:T(8,128)(2,1)S(1)}, bf16[16,2048]{1,0:T(8,128)(2,1)S(1)}, u32[]{:S(2)}, u32[]{:S(2)}) collective-permute-start(bf16[16,2048]{1,0:T(8,128)(2,1)S(1)} %get-tuple-element.65), channel_id=1, source_target_pairs={{0,8},{4,12},{8,0},{12,4},{16,24},{20,28},{24,16},{28,20},{32,40},... | collective-permute-start | bytes 196616 | tf_op jit(solution)/shard_map/ppermute | solution.py:300
  8.3 5.0 %collective-permute-start.1 = (bf16[16,2048]{1,0:T(8,128)(2,1)S(1)}, bf16[16,2048]{1,0:T(8,128)(2,1)S(1)}, u32[]{:S(2)}, u32[]{:S(2)}) collective-permute-start(bf16[16,2048]{1,0:T(8,128)(2,1)S(1)} %get-tuple-element.65), channel_id=1, source_target_pairs={{0,12},{4,8},{8,4},{12,0},{16,28},{20,24},{24,20},{28,16},{32,44},... | collective-permute-start | bytes 196616 | tf_op jit(solution)/shard_map/ppermute | solution.py:300
  9.1 4.2 %collective-permute-start.2 = (bf16[16,2048]{1,0:T(8,128)(2,1)S(1)}, bf16[16,2048]{1,0:T(8,128)(2,1)S(1)}, u32[]{:S(2)}, u32[]{:S(2)}) collective-permute-start(bf16[16,2048]{1,0:T(8,128)(2,1)S(1)} %get-tuple-element.65), channel_id=1, source_target_pairs={{0,4},{4,0},{8,12},{12,8},{16,20},{20,16},{24,28},{28,24},{32,36},... | collective-permute-start | bytes 196616 | tf_op jit(solution)/shard_map/ppermute | solution.py:300
  13.5 6.8 %collective-permute-start.3 = (bf16[16,2048]{1,0:T(8,128)(2,1)S(1)}, bf16[16,2048]{1,0:T(8,128)(2,1)S(1)}, u32[]{:S(2)}, u32[]{:S(2)}) collective-permute-start(bf16[16,2048]{1,0:T(8,128)(2,1)S(1)} %get-tuple-element.80), channel_id=1, source_target_pairs={{0,48},{4,52},{8,56},{12,60},{16,32},{20,36},{24,40},{28,44},{32,1... | collective-permute-start | bytes 196616 | tf_op jit(solution)/shard_map/ppermute | solution.py:300
  15.5 4.7 %collective-permute-start.4 = (bf16[16,2048]{1,0:T(8,128)(2,1)S(1)}, bf16[16,2048]{1,0:T(8,128)(2,1)S(1)}, u32[]{:S(2)}, u32[]{:S(2)}) collective-permute-start(bf16[16,2048]{1,0:T(8,128)(2,1)S(1)} %get-tuple-element.80), channel_id=1, source_target_pairs={{0,16},{4,20},{8,24},{12,28},{16,0},{20,4},{24,8},{28,12},{32,48},... | collective-permute-start | bytes 196616 | tf_op jit(solution)/shard_map/ppermute | solution.py:300
  15.7 4.6 %collective-permute-start.5 = (bf16[16,2048]{1,0:T(8,128)(2,1)S(1)}, bf16[16,2048]{1,0:T(8,128)(2,1)S(1)}, u32[]{:S(2)}, u32[]{:S(2)}) collective-permute-start(bf16[16,2048]{1,0:T(8,128)(2,1)S(1)} %get-tuple-element.80), channel_id=1, source_target_pairs={{0,32},{4,36},{8,40},{12,44},{16,48},{20,52},{24,56},{28,60},{32,0... | collective-permute-start | bytes 196616 | tf_op jit(solution)/shard_map/ppermute | solution.py:300
  20.4 11.0 %collective-permute-start.6 = (bf16[16,2048]{1,0:T(8,128)(2,1)S(1)}, bf16[16,2048]{1,0:T(8,128)(2,1)S(1)}, u32[]{:S(2)}, u32[]{:S(2)}) collective-permute-start(bf16[16,2048]{1,0:T(8,128)(2,1)S(1)} %get-tuple-element.93), channel_id=1, source_target_pairs={{0,160},{4,164},{8,168},{12,172},{16,176},{20,180},{24,184},{28,18... | collective-permute-start | bytes 196616 | tf_op jit(solution)/shard_map/ppermute | solution.py:300
  26.2 5.6 %collective-permute-start.7 = (bf16[16,2048]{1,0:T(8,128)(2,1)S(1)}, bf16[16,2048]{1,0:T(8,128)(2,1)S(1)}, u32[]{:S(2)}, u32[]{:S(2)}) collective-permute-start(bf16[16,2048]{1,0:T(8,128)(2,1)S(1)} %get-tuple-element.93), channel_id=1, source_target_pairs={{0,192},{4,196},{8,200},{12,204},{16,208},{20,212},{24,216},{28,22... | collective-permute-start | bytes 196616 | tf_op jit(solution)/shard_map/ppermute | solution.py:300
  26.5 5.6 %collective-permute-start.8 = (bf16[16,2048]{1,0:T(8,128)(2,1)S(1)}, bf16[16,2048]{1,0:T(8,128)(2,1)S(1)}, u32[]{:S(2)}, u32[]{:S(2)}) collective-permute-start(bf16[16,2048]{1,0:T(8,128)(2,1)S(1)} %get-tuple-element.93), channel_id=1, source_target_pairs={{0,64},{4,68},{8,72},{12,76},{16,80},{20,84},{24,88},{28,92},{32,9... | collective-permute-start | bytes 196616 | tf_op jit(solution)/shard_map/ppermute | solution.py:300
  35.2 4.7 %collective-permute-start.9 = (f32[1,256]{1,0:T(1,128)S(1)}, f32[1,256]{1,0:T(1,128)S(1)}, u32[]{:S(2)}, u32[]{:S(2)}) collective-permute-start(f32[1,256]{1,0:T(1,128)S(1)} %get-tuple-element.123), channel_id=1, source_target_pairs={{0,1},{1,0},{2,3},{3,2},{4,5},{5,4},{6,7},{7,6},{8,9},{9,8},{10,11... | collective-permute-start | bytes 3080 | tf_op jit(solution)/shard_map/ppermute | solution.py:323
  39.9 4.5 %collective-permute-start.10 = (f32[1,256]{1,0:T(1,128)S(1)}, f32[1,256]{1,0:T(1,128)S(1)}, u32[]{:S(2)}, u32[]{:S(2)}) collective-permute-start(f32[1,256]{1,0:T(1,128)S(1)} %add.3.mine_ref), channel_id=1, source_target_pairs={{0,3},{1,2},{2,1},{3,0},{4,7},{5,6},{6,5},{7,4},{8,11},{9,10},{10,... | collective-permute-start | bytes 3080 | tf_op jit(solution)/shard_map/ppermute | solution.py:324
  43.0 1.4 %copy-start = (f32[2048]{0:T(1024)S(1)}, f32[2048]{0:T(1024)}, u32[]{:S(2)}) copy-start(f32[2048]{0:T(1024)} %param.15) | copy-start | bytes 24580

commit v4 on v3

--- a/solution.py
+++ b/solution.py
@@ -154,12 +154,15 @@
         rest[2][...] = whole
 
 
-def finish_kernel(enter_ref, tile_ref, v_ref, *rest):
-    pieces = (len(rest) - 3) // 2
-    base_refs, lead_refs = rest[:pieces], rest[pieces:-3]
-    new_ref, power_ref, acc_ref = rest[-3:]
+def finish_kernel(size, order, decay_ref, one_ref, two_ref, three_ref, before_ref, tile_ref, v_ref, *rest):
+    pieces = (len(rest) - 4) // 2
+    base_refs, lead_refs = rest[:pieces], rest[pieces:-4]
+    new_ref, power_ref, acc_ref, enter_ref = rest[-4:]
     modes = tile_ref.shape[0]
     rows = v_ref.shape[0]
+    merge_kernel(
+        size, rows, order, False, True, decay_ref, None, one_ref, two_ref, three_ref, before_ref, enter_ref
+    )
     acc_ref[...] = jnp.zeros_like(acc_ref)
     for piece, (base_ref, lead_ref) in enumerate(zip(base_refs, lead_refs)):
 
@@ -304,21 +307,19 @@
         bases += [base for base, _ in made]
         leads += [lead for _, lead in made]
         last = level + 1 == len(stages)
-        merged = merge(4**level, order, last, total, arrived, enter)
-        enter = merged[0]
         if not last:
-            sent, total = merged[1:]
+            enter, sent, total = merge(4**level, order, last, total, arrived, enter)
 
     fresh, power = pl.pallas_call(
-        finish_kernel,
-        in_specs=[in_vmem] * (3 + 2 * pieces),
+        functools.partial(finish_kernel, 4**level, order),
+        in_specs=[in_vmem] * (7 + 2 * pieces),
         out_specs=[in_vmem] * 2,
         out_shape=[pltpu.VMEM((rows, width), bf16), pltpu.VMEM((1, rows), f32)],
-        scratch_shapes=[pltpu.VMEM((rows, lanes), f32)],
+        scratch_shapes=[pltpu.VMEM((rows, lanes), f32), pltpu.VMEM((modes, width), f32)],
         compiler_params=params,
         cost_estimate=pl.CostEstimate(flops=2 * modes * rows * width, bytes_accessed=8 * rows * width, transcendentals=0),
         name="finish",
-    )(enter, tile, near_values, *bases, *leads)
+    )(decay, *arrived, enter, tile, near_values, *bases, *leads)
 
     power = power + lax.ppermute(power, "tp", [(i, i ^ 1) for i in range(4)])
     other = lax.ppermute(power, "tp", [(i, i ^ 3) for i in range(4)])

time: 45.9 us -> 46.4 us (1.011)
  Pallas kernels: 19.2 us -> 19.8 us
    pallas_call x3 -> x2, Pallas kernels: 0.39 us -> 0.91 us  [merge(): pl.pallas_call(functools.partial(merge_kernel, size, rows, order, enter i...]
where the time goes in v4:
time: 46.4 us; the launch traced here: 46.3 us
  starting transfers between devices  21.2 us (46%)
  Pallas kernels  19.8 us (43%)
  waiting for transfers between devices  3.36 us (7%)
  local copies, waits for them, and re-layouts  0.97 us (2%)
  between operations  0.92 us (2%)
    ppermute x9, starting transfers between devices, shards(): arrived = [lax.ppermute(sent, 'ctx', links[at]) for at in order]  14.2 us
    pallas_call x8, Pallas kernels, local_piece(): pl.pallas_call(functools.partial(local_kernel, piece), in_specs=[in_vmem]...  10.7 us
    pallas_call x1, Pallas kernels, shards(): pl.pallas_call(state_kernel, in_specs=[anywhere] * len(far), out_specs=[i...  3.98 us
    ppermute x1, starting transfers between devices, shards(): power = power + lax.ppermute(power, 'tp', [(i, i ^ 1) for i in range(4)])  3.89 us
    ppermute x1, starting transfers between devices, shards(): other = lax.ppermute(power, 'tp', [(i, i ^ 3) for i in range(4)])  3.12 us
    pallas_call x1, Pallas kernels, shards(): pl.pallas_call(functools.partial(finish_kernel, 4 ** level, order), in_sp...  3.04 us
    ppermute x9, waiting for transfers between devices, shards(): arrived = [lax.ppermute(sent, 'ctx', links[at]) for at in order]  2.14 us
    pallas_call x1, Pallas kernels, shards(): pl.pallas_call(functools.partial(norm_kernel, channels), in_specs=[in_vme...  1.24 us
  transfers between devices with their start and end apart: 11, of which 5 were waited for; matrix products, arithmetic and copies ran while one was open for 2% of the time, Pallas kernels for 23%

profile of v4, /device:TPU:1, one launch (start us, length us, event | category | flops | bytes accessed | tf_op | source)
XLA Modules:
  0.0 46.3 jit_solution(11677587561390813077)
XLA Ops:
  0.6 4.0 %states.1 = (f32[16,2048]{1,0:T(8,128)S(1)}, bf16[16,2048]{1,0:T(8,128)(2,1)S(1)}, bf16[256,2048]{1,0:T(8,128)(2,1)S(1)}, bf16[256,2048]{1,0:T(8,128)(2,1)S(1)},...) custom-call(bf16[256,2048]{1,0:T(8,128)(2,1)} %q_hbm.1, ...), custom_call_target="tpu_custom_call" | custom-call | flops 16777216 | bytes 2097152 | tf_op jit(solution)/shard_map/states/pallas_call | solution.py:245
  4.6 3.7 %collective-permute-start = (bf16[16,2048]{1,0:T(8,128)(2,1)S(1)}, bf16[16,2048]{1,0:T(8,128)(2,1)S(1)}, u32[]{:S(2)}, u32[]{:S(2)}) collective-permute-start(bf16[16,2048]{1,0:T(8,128)(2,1)S(1)} %get-tuple-element.64), channel_id=1, source_target_pairs={{0,8},{4,12},{8,0},{12,4},{16,24},{20,28},{24,16},{28,20},{32,40},... | collective-permute-start | bytes 196616 | tf_op jit(solution)/shard_map/ppermute | solution.py:303
  8.3 0.9 %collective-permute-start.1 = (bf16[16,2048]{1,0:T(8,128)(2,1)S(1)}, bf16[16,2048]{1,0:T(8,128)(2,1)S(1)}, u32[]{:S(2)}, u32[]{:S(2)}) collective-permute-start(bf16[16,2048]{1,0:T(8,128)(2,1)S(1)} %get-tuple-element.64), channel_id=1, source_target_pairs={{0,12},{4,8},{8,4},{12,0},{16,28},{20,24},{24,20},{28,16},{32,44},... | collective-permute-start | bytes 196616 | tf_op jit(solution)/shard_map/ppermute | solution.py:303
  9.1 0.0 collective-permute-start.2
  9.1 1.3 %local.9 = (f32[256,256]{1,0:T(8,128)S(1)}, f32[16,8,256]{2,1,0:T(8,128)S(1)}) custom-call(f32[16,2048]{1,0:T(8,128)S(1)} %get-tuple-element.92.decay_ref, f32[16,2048]{1,0:T(8,128)S(1)} %get-tuple-element.66.res_ref, f32[1,2048]{1,0:T(1,128)S(1)} %get-tuple-element.67.skip_ref, bf16[256,2048]{1,0:T(8,128)(2,1)S(1)} %get-tuple-element.68.sig_ref, ...), custom_call_target="tpu_custom_call" | custom-call | flops 6291456 | bytes 786432 | tf_op jit(solution)/shard_map/local/pallas_call | solution.py:263
  10.5 1.3 %local.8 = (f32[256,256]{1,0:T(8,128)S(1)}, f32[16,8,256]{2,1,0:T(8,128)S(1)}) custom-call(f32[16,2048]{1,0:T(8,128)S(1)} %get-tuple-element.92.decay_ref, f32[16,2048]{1,0:T(8,128)S(1)} %get-tuple-element.66.res_ref, f32[1,2048]{1,0:T(1,128)S(1)} %get-tuple-element.67.skip_ref, bf16[256,2048]{1,0:T(8,128)(2,1)S(1)} %get-tuple-element.68.sig_ref, ...), custom_call_target="tpu_custom_call" | custom-call | flops 6291456 | bytes 786432 | tf_op jit(solution)/shard_map/local/pallas_call | solution.py:263
  11.8 0.0 collective-permute-done.rest_0_
  11.8 1.5 %collective-permute-done.1.rest_1_ = bf16[16,2048]{1,0:T(8,128)(2,1)S(1)} collective-permute-done((bf16[16,2048]{1,0:T(8,128)(2,1)S(1)}, bf16[16,2048]{1,0:T(8,128)(2,1)S(1)}, u32[]{:S(2)}, u32[]{:S(2)}) %collective-permute-start.1) | collective-permute-done | bytes 65568 | tf_op jit(solution)/shard_map/ppermute | solution.py:303
  13.3 0.0 collective-permute-done.2.rest_2_
  13.3 0.1 merge.2
  13.5 2.0 %collective-permute-start.3 = (bf16[16,2048]{1,0:T(8,128)(2,1)S(1)}, bf16[16,2048]{1,0:T(8,128)(2,1)S(1)}, u32[]{:S(2)}, u32[]{:S(2)}) collective-permute-start(bf16[16,2048]{1,0:T(8,128)(2,1)S(1)} %get-tuple-element.79), channel_id=1, source_target_pairs={{0,48},{4,52},{8,56},{12,60},{16,32},{20,36},{24,40},{28,44},{32,1... | collective-permute-start | bytes 196616 | tf_op jit(solution)/shard_map/ppermute | solution.py:303
  15.5 0.2 collective-permute-start.4
  15.7 0.5 %collective-permute-start.5 = (bf16[16,2048]{1,0:T(8,128)(2,1)S(1)}, bf16[16,2048]{1,0:T(8,128)(2,1)S(1)}, u32[]{:S(2)}, u32[]{:S(2)}) collective-permute-start(bf16[16,2048]{1,0:T(8,128)(2,1)S(1)} %get-tuple-element.79), channel_id=1, source_target_pairs={{0,32},{4,36},{8,40},{12,44},{16,48},{20,52},{24,56},{28,60},{32,0... | collective-permute-start | bytes 196616 | tf_op jit(solution)/shard_map/ppermute | solution.py:303
  16.2 1.3 %local.12 = (f32[256,256]{1,0:T(8,128)S(1)}, f32[16,8,256]{2,1,0:T(8,128)S(1)}) custom-call(f32[16,2048]{1,0:T(8,128)S(1)} %get-tuple-element.92.decay_ref, f32[16,2048]{1,0:T(8,128)S(1)} %get-tuple-element.66.res_ref, f32[1,2048]{1,0:T(1,128)S(1)} %get-tuple-element.67.skip_ref, bf16[256,2048]{1,0:T(8,128)(2,1)S(1)} %get-tuple-element.68.sig_ref, ...), custom_call_target="tpu_custom_call" | custom-call | flops 6291456 | bytes 786432 | tf_op jit(solution)/shard_map/local/pallas_call | solution.py:263
  17.5 1.3 %local.11 = (f32[256,256]{1,0:T(8,128)S(1)}, f32[16,8,256]{2,1,0:T(8,128)S(1)}) custom-call(f32[16,2048]{1,0:T(8,128)S(1)} %get-tuple-element.92.decay_ref, f32[16,2048]{1,0:T(8,128)S(1)} %get-tuple-element.66.res_ref, f32[1,2048]{1,0:T(1,128)S(1)} %get-tuple-element.67.skip_ref, bf16[256,2048]{1,0:T(8,128)(2,1)S(1)} %get-tuple-element.68.sig_ref, ...), custom_call_target="tpu_custom_call" | custom-call | flops 6291456 | bytes 786432 | tf_op jit(solution)/shard_map/local/pallas_call | solution.py:263
  18.9 1.3 %local.10 = (f32[256,256]{1,0:T(8,128)S(1)}, f32[16,8,256]{2,1,0:T(8,128)S(1)}) custom-call(f32[16,2048]{1,0:T(8,128)S(1)} %get-tuple-element.92.decay_ref, f32[16,2048]{1,0:T(8,128)S(1)} %get-tuple-element.66.res_ref, f32[1,2048]{1,0:T(1,128)S(1)} %get-tuple-element.67.skip_ref, bf16[256,2048]{1,0:T(8,128)(2,1)S(1)} %get-tuple-element.68.sig_ref, ...), custom_call_target="tpu_custom_call" | custom-call | flops 6291456 | bytes 786432 | tf_op jit(solution)/shard_map/local/pallas_call | solution.py:263
  20.2 0.0 collective-permute-done.3.rest_0_
  20.2 0.0 collective-permute-done.4.rest_1_
  20.2 0.0 collective-permute-done.5.rest_2_
  20.2 0.8 %merge.3 = (f32[16,2048]{1,0:T(8,128)S(1)}, bf16[16,2048]{1,0:T(8,128)(2,1)S(1)}, f32[16,2048]{1,0:T(8,128)}) custom-call(f32[16,2048]{1,0:T(8,128)S(1)} %get-tuple-element.92.decay_ref, f32[16,2048]{1,0:T(8,128)S(1)} %get-tuple-element.78.total_ref, bf16[16,2048]{1,0:T(8,128)(2,1)S(1)} %collective-permute-done.3.rest_0_, ...), custom_call_target="tpu_custom_call" | custom-call | tf_op jit(solution)/shard_map/merge/pallas_call | solution.py:290
  21.0 5.7 %collective-permute-start.6 = (bf16[16,2048]{1,0:T(8,128)(2,1)S(1)}, bf16[16,2048]{1,0:T(8,128)(2,1)S(1)}, u32[]{:S(2)}, u32[]{:S(2)}) collective-permute-start(bf16[16,2048]{1,0:T(8,128)(2,1)S(1)} %get-tuple-element.91), channel_id=1, source_target_pairs={{0,160},{4,164},{8,168},{12,172},{16,176},{20,180},{24,184},{28,18... | collective-permute-start | bytes 196616 | tf_op jit(solution)/shard_map/ppermute | solution.py:303
  26.8 0.3 collective-permute-start.7
  27.0 0.9 %collective-permute-start.8 = (bf16[16,2048]{1,0:T(8,128)(2,1)S(1)}, bf16[16,2048]{1,0:T(8,128)(2,1)S(1)}, u32[]{:S(2)}, u32[]{:S(2)}) collective-permute-start(bf16[16,2048]{1,0:T(8,128)(2,1)S(1)} %get-tuple-element.91), channel_id=1, source_target_pairs={{0,64},{4,68},{8,72},{12,76},{16,80},{20,84},{24,88},{28,92},{32,9... | collective-permute-start | bytes 196616 | tf_op jit(solution)/shard_map/ppermute | solution.py:303
  28.0 1.3 %local.15 = (f32[256,256]{1,0:T(8,128)S(1)}, f32[16,8,256]{2,1,0:T(8,128)S(1)}) custom-call(f32[16,2048]{1,0:T(8,128)S(1)} %get-tuple-element.92.decay_ref, f32[16,2048]{1,0:T(8,128)S(1)} %get-tuple-element.66.res_ref, f32[1,2048]{1,0:T(1,128)S(1)} %get-tuple-element.67.skip_ref, bf16[256,2048]{1,0:T(8,128)(2,1)S(1)} %get-tuple-element.68.sig_ref, ...), custom_call_target="tpu_custom_call" | custom-call | flops 6291456 | bytes 786432 | tf_op jit(solution)/shard_map/local/pallas_call | solution.py:263
  29.3 1.3 %local.14 = (f32[256,256]{1,0:T(8,128)S(1)}, f32[16,8,256]{2,1,0:T(8,128)S(1)}) custom-call(f32[16,2048]{1,0:T(8,128)S(1)} %get-tuple-element.92.decay_ref, f32[16,2048]{1,0:T(8,128)S(1)} %get-tuple-element.66.res_ref, f32[1,2048]{1,0:T(1,128)S(1)} %get-tuple-element.67.skip_ref, bf16[256,2048]{1,0:T(8,128)(2,1)S(1)} %get-tuple-element.68.sig_ref, ...), custom_call_target="tpu_custom_call" | custom-call | flops 6291456 | bytes 786432 | tf_op jit(solution)/shard_map/local/pallas_call | solution.py:263
  30.6 1.3 %local.13 = (f32[256,256]{1,0:T(8,128)S(1)}, f32[16,8,256]{2,1,0:T(8,128)S(1)}) custom-call(f32[16,2048]{1,0:T(8,128)S(1)} %get-tuple-element.92.decay_ref, f32[16,2048]{1,0:T(8,128)S(1)} %get-tuple-element.66.res_ref, f32[1,2048]{1,0:T(1,128)S(1)} %get-tuple-element.67.skip_ref, bf16[256,2048]{1,0:T(8,128)(2,1)S(1)} %get-tuple-element.68.sig_ref, ...), custom_call_target="tpu_custom_call" | custom-call | flops 6291456 | bytes 786432 | tf_op jit(solution)/shard_map/local/pallas_call | solution.py:263
  32.0 0.0 collective-permute-done.6.one_ref
  32.0 0.4 collective-permute-done.7.two_ref
  32.4 0.3 collective-permute-done.8.three_ref
  32.6 3.0 %finish.1 = (bf16[256,2048]{1,0:T(8,128)(2,1)S(1)}, f32[1,256]{1,0:T(1,128)S(1)}) custom-call(f32[16,2048]{1,0:T(8,128)S(1)} %get-tuple-element.92.decay_ref, bf16[16,2048]{1,0:T(8,128)(2,1)S(1)} %collective-permute-done.6.one_ref, bf16[16,2048]{1,0:T(8,128)(2,1)S(1)} %collective-permute-done.7.two_ref, ...), custom_call_target="tpu_custom_call" | custom-call | flops 16777216 | bytes 4194304 | tf_op jit(solution)/shard_map/finish/pallas_call | solution.py:313
  35.7 3.9 %collective-permute-start.9 = (f32[1,256]{1,0:T(1,128)S(1)}, f32[1,256]{1,0:T(1,128)S(1)}, u32[]{:S(2)}, u32[]{:S(2)}) collective-permute-start(f32[1,256]{1,0:T(1,128)S(1)} %get-tuple-element.121), channel_id=1, source_target_pairs={{0,1},{1,0},{2,3},{3,2},{4,5},{5,4},{6,7},{7,6},{8,9},{9,8},{10,11... | collective-permute-start | bytes 3080 | tf_op jit(solution)/shard_map/ppermute | solution.py:324
  39.6 0.8 %collective-permute-done.9 = f32[1,256]{1,0:T(1,128)S(1)} collective-permute-done((f32[1,256]{1,0:T(1,128)S(1)}, f32[1,256]{1,0:T(1,128)S(1)}, u32[]{:S(2)}, u32[]{:S(2)}) %collective-permute-start.9) | collective-permute-done | bytes 1056 | tf_op jit(solution)/shard_map/ppermute | solution.py:324
  40.4 3.1 %collective-permute-start.10 = (f32[1,256]{1,0:T(1,128)S(1)}, f32[1,256]{1,0:T(1,128)S(1)}, u32[]{:S(2)}, u32[]{:S(2)}) collective-permute-start(f32[1,256]{1,0:T(1,128)S(1)} %add.3.mine_ref), channel_id=1, source_target_pairs={{0,3},{1,2},{2,1},{3,0},{4,7},{5,6},{6,5},{7,4},{8,11},{9,10},{10,... | collective-permute-start | bytes 3080 | tf_op jit(solution)/shard_map/ppermute | solution.py:325
  43.5 0.0 copy-start
  43.5 1.0 %copy.10 = bf16[256,2048]{1,0:T(8,128)(2,1)} copy(bf16[256,2048]{1,0:T(8,128)(2,1)S(1)} %get-tuple-element.122.new_ref) | data formatting | bytes 2097152
  44.5 0.4 collective-permute-done.10.other_ref
  44.9 0.0 copy-done
  44.9 1.2 %normalise.1 = bf16[256,2048]{1,0:T(8,128)(2,1)} custom-call(f32[1,256]{1,0:T(1,128)S(1)} %add.3.mine_ref, f32[1,256]{1,0:T(1,128)S(1)} %collective-permute-done.10.other_ref, f32[1,2048]{1,0:T(1,128)S(1)} %bitcast.2, bf16[256,2048]{1,0:T(8,128)(2,1)S(1)} %get-tuple-element.122.new_ref), custom_call_target="tpu_custom_call" | custom-call | tf_op jit(solution)/shard_map/normalise/pallas_call | solution.py:328
  (1 shorter events, 0.0 us)
Async XLA Ops:
  4.6 7.2 %collective-permute-start = (bf16[16,2048]{1,0:T(8,128)(2,1)S(1)}, bf16[16,2048]{1,0:T(8,128)(2,1)S(1)}, u32[]{:S(2)}, u32[]{:S(2)}) collective-permute-start(bf16[16,2048]{1,0:T(8,128)(2,1)S(1)} %get-tuple-element.64), channel_id=1, source_target_pairs={{0,8},{4,12},{8,0},{12,4},{16,24},{20,28},{24,16},{28,20},{32,40},... | collective-permute-start | bytes 196616 | tf_op jit(solution)/shard_map/ppermute | solution.py:303
  8.3 5.0 %collective-permute-start.1 = (bf16[16,2048]{1,0:T(8,128)(2,1)S(1)}, bf16[16,2048]{1,0:T(8,128)(2,1)S(1)}, u32[]{:S(2)}, u32[]{:S(2)}) collective-permute-start(bf16[16,2048]{1,0:T(8,128)(2,1)S(1)} %get-tuple-element.64), channel_id=1, source_target_pairs={{0,12},{4,8},{8,4},{12,0},{16,28},{20,24},{24,20},{28,16},{32,44},... | collective-permute-start | bytes 196616 | tf_op jit(solution)/shard_map/ppermute | solution.py:303
  9.1 4.2 %collective-permute-start.2 = (bf16[16,2048]{1,0:T(8,128)(2,1)S(1)}, bf16[16,2048]{1,0:T(8,128)(2,1)S(1)}, u32[]{:S(2)}, u32[]{:S(2)}) collective-permute-start(bf16[16,2048]{1,0:T(8,128)(2,1)S(1)} %get-tuple-element.64), channel_id=1, source_target_pairs={{0,4},{4,0},{8,12},{12,8},{16,20},{20,16},{24,28},{28,24},{32,36},... | collective-permute-start | bytes 196616 | tf_op jit(solution)/shard_map/ppermute | solution.py:303
  13.5 6.8 %collective-permute-start.3 = (bf16[16,2048]{1,0:T(8,128)(2,1)S(1)}, bf16[16,2048]{1,0:T(8,128)(2,1)S(1)}, u32[]{:S(2)}, u32[]{:S(2)}) collective-permute-start(bf16[16,2048]{1,0:T(8,128)(2,1)S(1)} %get-tuple-element.79), channel_id=1, source_target_pairs={{0,48},{4,52},{8,56},{12,60},{16,32},{20,36},{24,40},{28,44},{32,1... | collective-permute-start | bytes 196616 | tf_op jit(solution)/shard_map/ppermute | solution.py:303
  15.5 4.7 %collective-permute-start.4 = (bf16[16,2048]{1,0:T(8,128)(2,1)S(1)}, bf16[16,2048]{1,0:T(8,128)(2,1)S(1)}, u32[]{:S(2)}, u32[]{:S(2)}) collective-permute-start(bf16[16,2048]{1,0:T(8,128)(2,1)S(1)} %get-tuple-element.79), channel_id=1, source_target_pairs={{0,16},{4,20},{8,24},{12,28},{16,0},{20,4},{24,8},{28,12},{32,48},... | collective-permute-start | bytes 196616 | tf_op jit(solution)/shard_map/ppermute | solution.py:303
  15.7 4.6 %collective-permute-start.5 = (bf16[16,2048]{1,0:T(8,128)(2,1)S(1)}, bf16[16,2048]{1,0:T(8,128)(2,1)S(1)}, u32[]{:S(2)}, u32[]{:S(2)}) collective-permute-start(bf16[16,2048]{1,0:T(8,128)(2,1)S(1)} %get-tuple-element.79), channel_id=1, source_target_pairs={{0,32},{4,36},{8,40},{12,44},{16,48},{20,52},{24,56},{28,60},{32,0... | collective-permute-start | bytes 196616 | tf_op jit(solution)/shard_map/ppermute | solution.py:303
  21.0 11.0 %collective-permute-start.6 = (bf16[16,2048]{1,0:T(8,128)(2,1)S(1)}, bf16[16,2048]{1,0:T(8,128)(2,1)S(1)}, u32[]{:S(2)}, u32[]{:S(2)}) collective-permute-start(bf16[16,2048]{1,0:T(8,128)(2,1)S(1)} %get-tuple-element.91), channel_id=1, source_target_pairs={{0,160},{4,164},{8,168},{12,172},{16,176},{20,180},{24,184},{28,18... | collective-permute-start | bytes 196616 | tf_op jit(solution)/shard_map/ppermute | solution.py:303
  26.8 5.6 %collective-permute-start.7 = (bf16[16,2048]{1,0:T(8,128)(2,1)S(1)}, bf16[16,2048]{1,0:T(8,128)(2,1)S(1)}, u32[]{:S(2)}, u32[]{:S(2)}) collective-permute-start(bf16[16,2048]{1,0:T(8,128)(2,1)S(1)} %get-tuple-element.91), channel_id=1, source_target_pairs={{0,192},{4,196},{8,200},{12,204},{16,208},{20,212},{24,216},{28,22... | collective-permute-start | bytes 196616 | tf_op jit(solution)/shard_map/ppermute | solution.py:303
  27.0 5.6 %collective-permute-start.8 = (bf16[16,2048]{1,0:T(8,128)(2,1)S(1)}, bf16[16,2048]{1,0:T(8,128)(2,1)S(1)}, u32[]{:S(2)}, u32[]{:S(2)}) collective-permute-start(bf16[16,2048]{1,0:T(8,128)(2,1)S(1)} %get-tuple-element.91), channel_id=1, source_target_pairs={{0,64},{4,68},{8,72},{12,76},{16,80},{20,84},{24,88},{28,92},{32,9... | collective-permute-start | bytes 196616 | tf_op jit(solution)/shard_map/ppermute | solution.py:303
  35.7 4.7 %collective-permute-start.9 = (f32[1,256]{1,0:T(1,128)S(1)}, f32[1,256]{1,0:T(1,128)S(1)}, u32[]{:S(2)}, u32[]{:S(2)}) collective-permute-start(f32[1,256]{1,0:T(1,128)S(1)} %get-tuple-element.121), channel_id=1, source_target_pairs={{0,1},{1,0},{2,3},{3,2},{4,5},{5,4},{6,7},{7,6},{8,9},{9,8},{10,11... | collective-permute-start | bytes 3080 | tf_op jit(solution)/shard_map/ppermute | solution.py:324
  40.4 4.5 %collective-permute-start.10 = (f32[1,256]{1,0:T(1,128)S(1)}, f32[1,256]{1,0:T(1,128)S(1)}, u32[]{:S(2)}, u32[]{:S(2)}) collective-permute-start(f32[1,256]{1,0:T(1,128)S(1)} %add.3.mine_ref), channel_id=1, source_target_pairs={{0,3},{1,2},{2,1},{3,0},{4,7},{5,6},{6,5},{7,4},{8,11},{9,10},{10,... | collective-permute-start | bytes 3080 | tf_op jit(solution)/shard_map/ppermute | solution.py:325
  43.5 1.4 %copy-start = (f32[2048]{0:T(1024)S(1)}, f32[2048]{0:T(1024)}, u32[]{:S(2)}) copy-start(f32[2048]{0:T(1024)} %param.15) | copy-start | bytes 24580
